TPU v7x, 128 devices: a whole 4x4x4 slice. The times are simulated.
128 devices in a mesh: dp: 8 (over y, x_hi), seq: 16 (over x_lo, z, core).
Axes of the slice: x: 4 (x_hi: 2, x_lo: 2; x = x_hi * 2 + x_lo), y: 4, z: 4, core: 2. Of those that a mesh axis runs over, the one named last changes fastest.
Arguments:
- queries: bfloat16 [8, 16, 256, 40, 128], P('dp', 'seq'), may hold values from -6 to 6
- key_proj: bfloat16 [8, 16, 256, 40, 128], P('dp', 'seq'), may hold values from -6 to 6
- value_proj: bfloat16 [8, 16, 256, 40, 128], P('dp', 'seq'), may hold values from -6 to 6
- out_grad: bfloat16 [8, 16, 256, 40, 128], P('dp', 'seq'), may hold values from -6 to 6
- query_gain: float32 [40, 128], P('dp'), may hold values from 0.5 to 5
- key_gain: float32 [40, 128], P('dp'), may hold values from 0.5 to 5
Outputs:
- query_grad: bfloat16 [8, 16, 256, 40, 128], P('dp', 'seq')
- key_grad: bfloat16 [8, 16, 256, 40, 128], P('dp', 'seq')
- value_grad: bfloat16 [8, 16, 256, 40, 128], P('dp', 'seq')
- query_gain_grad: float32 [40, 128], P('dp')
- key_gain_grad: float32 [40, 128], P('dp')
All inputs are finite; a program needn't handle non-finite values.
Results may differ from a plain program's by a relative error of at most 0.0034.
The roundings to bfloat16 on the way count: a program that leaves them out, or rounds other values in their place, can miss the bound.
Values may be sent and summed in bfloat16 or wider, within the bound.
A program may use at most 128 MiB of HBM per device.

v0:
```python
import math

import jax
import jax.numpy as jnp
from jax import lax
from jax.sharding import PartitionSpec as P

EPSILON = 1e-06


def normalize(values):
    wide = values.astype(jnp.float32)
    inverse = lax.rsqrt(jnp.mean(wide * wide, axis=-1, keepdims=True) + EPSILON)
    return (wide * inverse, inverse)


def norm_back(step, hat, inverse, gain):
    step_wide = step.astype(jnp.float32)
    gained = gain * step_wide
    result = (inverse * (gained - hat * jnp.mean(gained * hat, axis=-1, keepdims=True))).astype(
        jnp.bfloat16
    )
    gain_part = jnp.sum(step_wide * hat, axis=tuple(range(step.ndim - 2)))
    return (result, gain_part)


def attention_grads(query_norm, key_norm, value_in, grad_in):
    frames = query_norm.shape[1]
    scaling = 1.0 / math.sqrt(query_norm.shape[-1])
    scores = (
        jnp.einsum("efphd,egphd->ephfg", query_norm, key_norm, preferred_element_type=jnp.float32)
        * scaling
    )
    row_ids = lax.broadcasted_iota(jnp.int32, (frames, frames), 0)
    col_ids = lax.broadcasted_iota(jnp.int32, (frames, frames), 1)
    allowed = col_ids <= row_ids
    scores = jnp.where(allowed, scores, -jnp.inf)
    largest = jnp.max(scores, axis=-1, keepdims=True)
    expo = jnp.exp(scores - largest)
    probability = expo / jnp.sum(expo, axis=-1, keepdims=True)
    prob_low = probability.astype(jnp.bfloat16)
    attn_out = jnp.einsum(
        "ephfg,egphd->efphd", prob_low, value_in, preferred_element_type=jnp.float32
    )
    row_dots = jnp.transpose(jnp.sum(grad_in.astype(jnp.float32) * attn_out, axis=-1), (0, 2, 3, 1))
    prob_grad = jnp.einsum(
        "efphd,egphd->ephfg", grad_in, value_in, preferred_element_type=jnp.float32
    )
    score_low = (probability * (prob_grad - row_dots[..., None])).astype(jnp.bfloat16)
    query_step = (
        jnp.einsum("ephfg,egphd->efphd", score_low, key_norm, preferred_element_type=jnp.float32)
        * scaling
    ).astype(jnp.bfloat16)
    key_step = (
        jnp.einsum("ephfg,efphd->egphd", score_low, query_norm, preferred_element_type=jnp.float32)
        * scaling
    ).astype(jnp.bfloat16)
    value_step = jnp.einsum(
        "ephfg,efphd->egphd", prob_low, grad_in, preferred_element_type=jnp.float32
    ).astype(jnp.bfloat16)
    return (query_step, key_step, value_step)


def body(queries, key_proj, value_proj, out_grad, query_gain, key_gain):
    query_gains, key_gains = (
        lax.all_gather(query_gain, "dp", axis=0, tiled=True),
        lax.all_gather(key_gain, "dp", axis=0, tiled=True),
    )
    query_hat, query_inverse = normalize(queries)
    key_hat, key_inverse = normalize(key_proj)
    query_norm = (query_hat * query_gains).astype(jnp.bfloat16)
    key_norm = (key_hat * key_gains).astype(jnp.bfloat16)
    pieces = (
        lax.all_to_all(query_norm, "seq", split_axis=2, concat_axis=1, tiled=True),
        lax.all_to_all(key_norm, "seq", split_axis=2, concat_axis=1, tiled=True),
        lax.all_to_all(value_proj, "seq", split_axis=2, concat_axis=1, tiled=True),
        lax.all_to_all(out_grad, "seq", split_axis=2, concat_axis=1, tiled=True),
    )
    query_local, key_local, value_local = attention_grads(
        pieces[0], pieces[1], pieces[2], pieces[3]
    )
    query_step, key_step, value_step = (
        lax.all_to_all(query_local, "seq", split_axis=1, concat_axis=2, tiled=True),
        lax.all_to_all(key_local, "seq", split_axis=1, concat_axis=2, tiled=True),
        lax.all_to_all(value_local, "seq", split_axis=1, concat_axis=2, tiled=True),
    )
    query_grad, query_part = norm_back(query_step, query_hat, query_inverse, query_gains)
    key_grad, key_part = norm_back(key_step, key_hat, key_inverse, key_gains)
    totals = lax.psum((query_part, key_part), "seq")
    query_total, key_total = (
        lax.psum_scatter(totals[0], "dp", scatter_dimension=0, tiled=True),
        lax.psum_scatter(totals[1], "dp", scatter_dimension=0, tiled=True),
    )
    return (query_grad, key_grad, value_step, query_total, key_total)


def solution(mesh):
    in_specs = (
        P("dp", "seq", None, None, None),
        P("dp", "seq", None, None, None),
        P("dp", "seq", None, None, None),
        P("dp", "seq", None, None, None),
        P("dp", None),
        P("dp", None),
    )
    out_specs = (
        P("dp", "seq", None, None, None),
        P("dp", "seq", None, None, None),
        P("dp", "seq", None, None, None),
        P("dp", None),
        P("dp", None),
    )
    return jax.shard_map(body, mesh=mesh, in_specs=in_specs, out_specs=out_specs, check_vma=False)
```

profile of v0, /device:TPU:1, one launch (start us, length us, event | category | flops | bytes accessed | tf_op | source)
XLA Modules:
  0.0 457.2 jit_solution(17062742028848093395)
XLA Ops:
  3.8 29.0 %all-gather.1 = f32[8,5,128]{2,1,0:T(8,128)S(1)} all-gather(f32[1,5,128]{2,1,0:T(8,128)} %bitcast.64), channel_id=1, replica_groups=mesh['dp'=8,'seq'=16] {'dp'}, dimensions={0}, use_global_device_ids=true | all-gather | bytes 23040 | tf_op jit(solution)/shard_map/all_gather | solution.py:67
  32.9 5.0 %fusion.25 = bf16[1,1,256,40,128]{4,3,1,0,2:T(8,128)(2,1)} fusion(bf16[1,1,256,40,128]{4,3,2,1,0:T(8,128)(2,1)} %param.7, f32[40,128]{1,0:T(8,128)S(1)} %reshape.219, f32[256,40]{1,0:T(8,128)S(1)} %add_rsqrt_fusion), kind=kLoop, calls=%fused_computation.39 | loop fusion | flops 5242880 | bytes 5304320 | tf_op jit(solution)/shard_map/convert_element_type | solution.py:72
  37.9 13.3 %all-to-all-start = ((bf16[1,1,256,40,128]{4,3,1,0,2:T(8,128)(2,1)}), bf16[1,1,256,40,128]{4,3,1,0,2:T(8,128)(2,1)}, u32[]{:S(2)}, u32[]{:S(2)}) async-start(bf16[1,1,256,40,128]{4,3,1,0,2:T(8,128)(2,1)} %fusion.25), calls=%async_computation | async-start | bytes 5242880 | tf_op jit(solution)/shard_map/all_to_all | solution.py:75
  51.2 58.7 %all-gather = f32[8,5,128]{2,1,0:T(8,128)S(1)} all-gather(f32[1,5,128]{2,1,0:T(8,128)S(1)} %bitcast.65), channel_id=1, replica_groups=mesh['dp'=8,'seq'=16] {'dp'}, dimensions={0}, use_global_device_ids=true | all-gather | bytes 23040 | tf_op jit(solution)/shard_map/all_gather | solution.py:66
  114.5 44.2 %all_to_all.31 = bf16[1,1,256,40,128]{4,3,1,0,2:T(8,128)(2,1)S(1)} all-to-all(bf16[1,1,256,40,128]{4,3,1,0,2:T(8,128)(2,1)} %fusion.26), channel_id=1, replica_groups=mesh['dp'=8,'seq'=16] {'seq'}, dimensions={2} | all-to-all | bytes 5242880 | tf_op jit(solution)/shard_map/all_to_all | solution.py:74
  158.7 37.8 %all_to_all.32 = bf16[1,1,256,40,128]{4,3,1,0,2:T(8,128)(2,1)} all-to-all(bf16[1,1,256,40,128]{4,3,1,0,2:T(8,128)(2,1)} %bitcast.62), channel_id=1, replica_groups=mesh['dp'=8,'seq'=16] {'seq'}, dimensions={2} | all-to-all | bytes 5242880 | tf_op jit(solution)/shard_map/all_to_all | solution.py:77
  196.5 5.4 %all-to-all-start.3 = ((bf16[1,1,256,40,128]{4,3,1,0,2:T(8,128)(2,1)}), bf16[1,1,256,40,128]{4,3,1,0,2:T(8,128)(2,1)}, u32[]{:S(2)}, u32[]{:S(2)}) async-start(bf16[1,1,256,40,128]{4,3,1,0,2:T(8,128)(2,1)} %bitcast.63), calls=%async_computation.3 | async-start | bytes 5242880 | tf_op jit(solution)/shard_map/all_to_all | solution.py:76
  206.5 4.9 %fusion.30 = f32[16,40,16,16]{2,3,1,0:T(8,128)S(1)} fusion(bf16[16,16,40,128]{3,2,1,0:T(8,128)(2,1)} %bitcast.3, bf16[16,16,40,128]{3,2,1,0:T(8,128)(2,1)S(1)} %bitcast.57), kind=kOutput, calls=%fused_computation.46 | convolution fusion | flops 41943040 | bytes 5898240 | tf_op jit(solution)/shard_map/efphd,egphd->ephfg/dot_general | solution.py:31
  215.5 20.2 %all-to-all-done.3 = bf16[1,1,256,40,128]{4,3,1,0,2:T(8,128)(2,1)} async-done(((bf16[1,1,256,40,128]{4,3,1,0,2:T(8,128)(2,1)}), bf16[1,1,256,40,128]{4,3,1,0,2:T(8,128)(2,1)}, u32[]{:S(2)}, u32[]{:S(2)}) %all-to-all-start.3) | async-done | bytes 2621472 | tf_op jit(solution)/shard_map/all_to_all | solution.py:76
  235.7 10.9 %fusion.21 = f32[16,16,40]{0,2,1:T(8,128)S(1)} fusion(f32[1,16,16,40,128]{4,3,2,1,0:T(8,128)} %convert.5, bf16[16,16,40,128]{3,2,1,0:T(8,128)(2,1)} %bitcast.9, f32[16,40,16,16]{2,3,1,0:T(8,128)} %get-tuple-element.14, f32[16,40,16]{2,1,0:T(8,128)S(1)} %get-tuple-element.13), kind=kOutput, calls=%fused_computation.30 | convolution fusion | flops 44881920 | bytes 8601600 | tf_op jit(solution)/shard_map/ephfg,egphd->efphd/dot_general | solution.py:42
  246.6 5.5 %multiply_convert_fusion.2 = bf16[16,40,16,16]{2,3,1,0:T(8,128)(2,1)S(1)} fusion(f32[16,40,16]{2,1,0:T(8,128)S(1)} %bitcast.66, bf16[16,16,40,128]{3,2,1,0:T(8,128)(2,1)} %bitcast.9, bf16[16,16,40,128]{3,2,1,0:T(8,128)(2,1)S(1)} %bitcast.61, f32[16,40,16,16]{2,3,1,0:T(8,128)S(1)} %copy-done.9, f32[16,40,16]{2,1,0:T(8,128)S(1)} %get-tuple-element.13), kind=kOutput, calls=%fused_computation.33 | convolution fusion | flops 42598400 | bytes 6307840 | tf_op jit(solution)/shard_map/efphd,egphd->ephfg/dot_general | solution.py:46
  256.3 8.5 %all-to-all-start.5 = ((bf16[1,16,16,40,128]{4,3,2,0,1:T(8,128)(2,1)}), bf16[1,16,16,40,128]{4,3,2,0,1:T(8,128)(2,1)S(1)}, u32[]{:S(2)}, u32[]{:S(2)}) async-start(bf16[1,16,16,40,128]{4,3,2,0,1:T(8,128)(2,1)} %copy.47), calls=%async_computation.5 | async-start | bytes 5242880 | tf_op jit(solution)/shard_map/all_to_all | solution.py:84
  271.6 26.7 %all-to-all-done.5 = bf16[1,16,16,40,128]{4,3,2,0,1:T(8,128)(2,1)S(1)} async-done(((bf16[1,16,16,40,128]{4,3,2,0,1:T(8,128)(2,1)}), bf16[1,16,16,40,128]{4,3,2,0,1:T(8,128)(2,1)S(1)}, u32[]{:S(2)}, u32[]{:S(2)}) %all-to-all-start.5) | async-done | bytes 2621472 | tf_op jit(solution)/shard_map/all_to_all | solution.py:84
  298.3 8.9 %all-to-all-start.4 = ((bf16[1,16,16,40,128]{4,3,2,0,1:T(8,128)(2,1)}), bf16[1,16,16,40,128]{4,3,2,0,1:T(8,128)(2,1)}, u32[]{:S(2)}, u32[]{:S(2)}) async-start(bf16[1,16,16,40,128]{4,3,2,0,1:T(8,128)(2,1)} %copy.44), calls=%async_computation.4 | async-start | bytes 5242880 | tf_op jit(solution)/shard_map/all_to_all | solution.py:83
  308.5 5.4 %convert_bitcast_fusion = bf16[1,16,16,40,128]{4,1,3,2,0:T(8,128)(2,1)S(1)} fusion(bf16[16,16,40,128]{3,2,1,0:T(8,128)(2,1)} %bitcast.60, f32[16,40,16,16]{2,3,1,0:T(8,128)} %get-tuple-element.14, f32[16,40,16]{2,1,0:T(8,128)S(1)} %get-tuple-element.13), kind=kOutput, calls=%fused_computation.41 | convolution fusion | flops 43581440 | bytes 5939200 | tf_op jit(solution)/shard_map/ephfg,efphd->egphd/dot_general | solution.py:58
  316.1 24.9 %all-to-all-done.4 = bf16[1,16,16,40,128]{4,3,2,0,1:T(8,128)(2,1)} async-done(((bf16[1,16,16,40,128]{4,3,2,0,1:T(8,128)(2,1)}), bf16[1,16,16,40,128]{4,3,2,0,1:T(8,128)(2,1)}, u32[]{:S(2)}, u32[]{:S(2)}) %all-to-all-start.4) | async-done | bytes 2621472 | tf_op jit(solution)/shard_map/all_to_all | solution.py:83
  340.9 8.9 %all-to-all-start.6 = ((bf16[1,16,16,40,128]{4,3,2,0,1:T(8,128)(2,1)}), bf16[1,16,16,40,128]{4,3,2,0,1:T(8,128)(2,1)}, u32[]{:S(2)}, u32[]{:S(2)}) async-start(bf16[1,16,16,40,128]{4,3,2,0,1:T(8,128)(2,1)} %copy.50), calls=%async_computation.6 | async-start | bytes 5242880 | tf_op jit(solution)/shard_map/all_to_all | solution.py:85
  349.8 5.2 %fusion.20 = (f32[40,128]{1,0:T(8,128)S(1)}, f32[256,40]{1,0:T(8,128)S(1)}) fusion(bf16[1,1,256,40,128]{4,3,2,1,0:T(8,128)(2,1)S(1)} %copy-done, bf16[1,1,256,40,128]{4,3,2,1,0:T(8,128)(2,1)} %bitcast.55, f32[256,40]{1,0:T(8,128)S(1)} %add_rsqrt_fusion, f32[40,128]{1,0:T(8,128)S(1)} %reshape.219), kind=kLoop, calls=%fused_computation.28 | loop fusion | flops 10470400 | bytes 5365760 | tf_op jit(solution)/shard_map/reduce_sum | solution.py:23
  355.1 5.1 %fusion.19 = (f32[40,128]{1,0:T(8,128)S(1)}, f32[256,40]{1,0:T(8,128)S(1)}) fusion(bf16[1,1,256,40,128]{4,3,2,1,0:T(8,128)(2,1)S(1)} %copy-done.2, bf16[1,1,256,40,128]{4,3,2,1,0:T(8,128)(2,1)} %bitcast.30, f32[256,40]{1,0:T(8,128)S(1)} %add_rsqrt_fusion.1, f32[40,128]{1,0:T(8,128)S(1)} %reshape.217), kind=kLoop, calls=%fused_computation.27 | loop fusion | flops 10470400 | bytes 5365760 | tf_op jit(solution)/shard_map/reduce_sum | solution.py:23
  360.2 5.0 %fusion.10 = bf16[1,1,256,40,128]{4,3,2,1,0:T(8,128)(2,1)} fusion(bf16[1,1,256,40,128]{4,3,2,1,0:T(8,128)(2,1)S(1)} %bitcast.56, bf16[1,1,256,40,128]{4,3,2,1,0:T(8,128)(2,1)S(1)} %copy-done, f32[256,40]{1,0:T(8,128)S(1)} %broadcast_multiply_fusion, f32[40,128]{1,0:T(8,128)S(1)} %reshape.219, f32[256,40]{1,0:T(8,128)S(1)} %add_rsqrt_fusion), kind=kLoop, calls=%fused_computation.18 | loop fusion | flops 10485760 | bytes 7966720 | tf_op jit(solution)/shard_map/convert_element_type | solution.py:20
  365.2 6.2 %fusion.12 = bf16[1,1,256,40,128]{4,3,2,1,0:T(8,128)(2,1)} fusion(bf16[1,1,256,40,128]{4,3,2,1,0:T(8,128)(2,1)} %bitcast.30, bf16[1,1,256,40,128]{4,3,2,1,0:T(8,128)(2,1)S(1)} %copy-done.2, f32[256,40]{1,0:T(8,128)S(1)} %broadcast_multiply_fusion.1, f32[40,128]{1,0:T(8,128)S(1)} %reshape.217, f32[256,40]{1,0:T(8,128)S(1)} %add_rsqrt_fusion.1), kind=kLoop, calls=%fused_computation.20 | loop fusion | flops 10485760 | bytes 7966720 | tf_op jit(solution)/shard_map/convert_element_type | solution.py:20
  371.4 12.1 %all-to-all-done.6 = bf16[1,16,16,40,128]{4,3,2,0,1:T(8,128)(2,1)} async-done(((bf16[1,16,16,40,128]{4,3,2,0,1:T(8,128)(2,1)}), bf16[1,16,16,40,128]{4,3,2,0,1:T(8,128)(2,1)}, u32[]{:S(2)}, u32[]{:S(2)}) %all-to-all-start.6) | async-done | bytes 2621472 | tf_op jit(solution)/shard_map/all_to_all | solution.py:85
  383.5 32.2 %all-reduce.3 = (f32[40,128]{1,0:T(8,128)S(1)}, f32[40,128]{1,0:T(8,128)S(1)}) all-reduce(f32[40,128]{1,0:T(8,128)S(1)} %get-tuple-element.7, f32[40,128]{1,0:T(8,128)S(1)} %get-tuple-element.5), channel_id=2, replica_groups=mesh['dp'=8,'seq'=16] {'dp'}, use_global_device_ids=true, to_apply=%region_9.10.clone | all-reduce | flops 10240 | bytes 81920
  415.8 37.8 %all-reduce.2 = (f32[5,128]{1,0:T(8,128)}, f32[5,128]{1,0:T(8,128)}) all-reduce(f32[5,128]{1,0:T(8,128)S(1)} %get-tuple-element.16, f32[5,128]{1,0:T(8,128)S(1)} %get-tuple-element.15), channel_id=1, replica_groups=mesh['dp'=8,'seq'=16] {'seq'}, use_global_device_ids=true, to_apply=%region_8.9 | all-reduce | flops 1280 | bytes 10240 | tf_op jit(solution)/shard_map/psum | solution.py:89
  (41 shorter events, 34.2 us)
Async XLA Ops:
  32.9 18.3 %copy-start.7 = (f32[5,128]{1,0:T(8,128)S(1)}, f32[5,128]{1,0:T(8,128)}, u32[]{:S(2)}) copy-start(f32[5,128]{1,0:T(8,128)} %param.10) | copy-start | bytes 7684
  32.9 77.0 %copy-start.1 = (bf16[1,1,256,40,128]{4,3,2,1,0:T(8,128)(2,1)S(1)}, bf16[1,1,256,40,128]{4,3,2,1,0:T(8,128)(2,1)}, u32[]{:S(2)}) copy-start(bf16[1,1,256,40,128]{4,3,2,1,0:T(8,128)(2,1)} %param.6) | copy-start | bytes 7864324
  37.9 76.6 %all-to-all-start = ((bf16[1,1,256,40,128]{4,3,1,0,2:T(8,128)(2,1)}), bf16[1,1,256,40,128]{4,3,1,0,2:T(8,128)(2,1)}, u32[]{:S(2)}, u32[]{:S(2)}) async-start(bf16[1,1,256,40,128]{4,3,1,0,2:T(8,128)(2,1)} %fusion.25), calls=%async_computation | async-start | bytes 5242880 | tf_op jit(solution)/shard_map/all_to_all | solution.py:75
  196.5 39.2 %all-to-all-start.3 = ((bf16[1,1,256,40,128]{4,3,1,0,2:T(8,128)(2,1)}), bf16[1,1,256,40,128]{4,3,1,0,2:T(8,128)(2,1)}, u32[]{:S(2)}, u32[]{:S(2)}) async-start(bf16[1,1,256,40,128]{4,3,1,0,2:T(8,128)(2,1)} %bitcast.63), calls=%async_computation.3 | async-start | bytes 5242880 | tf_op jit(solution)/shard_map/all_to_all | solution.py:76
  235.7 10.9 %copy-start.5 = (bf16[1,1,256,40,128]{4,3,1,0,2:T(8,128)(2,1)S(1)}, bf16[1,1,256,40,128]{4,3,1,0,2:T(8,128)(2,1)}, u32[]{:S(2)}) copy-start(bf16[1,1,256,40,128]{4,3,1,0,2:T(8,128)(2,1)} %all_to_all.32) | copy-start | bytes 7864324
  235.7 10.9 %copy-start.9 = (f32[16,40,16,16]{2,3,1,0:T(8,128)S(1)}, f32[16,40,16,16]{2,3,1,0:T(8,128)}, u32[]{:S(2)}) copy-start(f32[16,40,16,16]{2,3,1,0:T(8,128)} %get-tuple-element.14) | copy-start | bytes 1966084
  252.1 2.0 copy-start.6
  256.3 42.1 %all-to-all-start.5 = ((bf16[1,16,16,40,128]{4,3,2,0,1:T(8,128)(2,1)}), bf16[1,16,16,40,128]{4,3,2,0,1:T(8,128)(2,1)S(1)}, u32[]{:S(2)}, u32[]{:S(2)}) async-start(bf16[1,16,16,40,128]{4,3,2,0,1:T(8,128)(2,1)} %copy.47), calls=%async_computation.5 | async-start | bytes 5242880 | tf_op jit(solution)/shard_map/all_to_all | solution.py:84
  269.4 37.8 %copy-start.8 = (u32[128]{0:T(128)S(1)}, u32[128]{0:T(128)}, u32[]{:S(2)}) copy-start(u32[128]{0:T(128)} %constant.23) | copy-start | bytes 1540
  298.3 10.1 %copy-start.3 = (bf16[1,16,16,40,128]{4,3,2,0,1:T(8,128)(2,1)}, bf16[1,16,16,40,128]{4,3,2,0,1:T(8,128)(2,1)S(1)}, u32[]{:S(2)}) copy-start(bf16[1,16,16,40,128]{4,3,2,0,1:T(8,128)(2,1)S(1)} %all-to-all-done.5) | copy-start | bytes 7864324
  298.3 42.6 %all-to-all-start.4 = ((bf16[1,16,16,40,128]{4,3,2,0,1:T(8,128)(2,1)}), bf16[1,16,16,40,128]{4,3,2,0,1:T(8,128)(2,1)}, u32[]{:S(2)}, u32[]{:S(2)}) async-start(bf16[1,16,16,40,128]{4,3,2,0,1:T(8,128)(2,1)} %copy.44), calls=%async_computation.4 | async-start | bytes 5242880 | tf_op jit(solution)/shard_map/all_to_all | solution.py:83
  313.8 36.0 %copy-start = (bf16[1,1,256,40,128]{4,3,2,1,0:T(8,128)(2,1)S(1)}, bf16[1,1,256,40,128]{4,3,2,1,0:T(8,128)(2,1)}, u32[]{:S(2)}) copy-start(bf16[1,1,256,40,128]{4,3,2,1,0:T(8,128)(2,1)} %param.7) | copy-start | bytes 7864324
  340.9 42.6 %all-to-all-start.6 = ((bf16[1,16,16,40,128]{4,3,2,0,1:T(8,128)(2,1)}), bf16[1,16,16,40,128]{4,3,2,0,1:T(8,128)(2,1)}, u32[]{:S(2)}, u32[]{:S(2)}) async-start(bf16[1,16,16,40,128]{4,3,2,0,1:T(8,128)(2,1)} %copy.50), calls=%async_computation.6 | async-start | bytes 5242880 | tf_op jit(solution)/shard_map/all_to_all | solution.py:85
  349.8 5.3 %copy-start.2 = (bf16[1,1,256,40,128]{4,3,2,1,0:T(8,128)(2,1)S(1)}, bf16[1,1,256,40,128]{4,3,2,1,0:T(8,128)(2,1)}, u32[]{:S(2)}) copy-start(bf16[1,1,256,40,128]{4,3,2,1,0:T(8,128)(2,1)} %param.6) | copy-start | bytes 7864324
  349.8 10.4 %copy-start.4 = (bf16[1,16,16,40,128]{4,3,2,0,1:T(8,128)(2,1)S(1)}, bf16[1,16,16,40,128]{4,3,2,0,1:T(8,128)(2,1)}, u32[]{:S(2)}) copy-start(bf16[1,16,16,40,128]{4,3,2,0,1:T(8,128)(2,1)} %copy-done.3) | copy-start | bytes 7864324
where the time goes:
time: 458 us; the launch traced here: 457 us
  blocking collectives  240 us (52%)
  waiting for transfers between devices  83.9 us (18%)
  starting transfers between devices  44.8 us (10%)
  other arithmetic  43.1 us (9%)
  matrix products  33.3 us (7%)
  local copies, waits for them, and re-layouts  10.9 us (2%)
    all_gather x1, blocking collectives, body(): lax.all_gather(query_gain, 'dp', axis=0, tiled=True)  58.7 us
    all_to_all x1, blocking collectives, body(): lax.all_to_all(query_norm, 'seq', split_axis=2, concat_axis=1, tiled=True)  44.2 us
    all_to_all x1, blocking collectives, body(): lax.all_to_all(out_grad, 'seq', split_axis=2, concat_axis=1, tiled=True)  37.8 us
    psum x1, blocking collectives, body(): totals = lax.psum((query_part, key_part), 'seq')  37.8 us
    unnamed x1, blocking collectives  32.2 us
    all_gather x1, blocking collectives, body(): lax.all_gather(key_gain, 'dp', axis=0, tiled=True)  29 us
    all_to_all x1, waiting for transfers between devices, body(): lax.all_to_all(key_local, 'seq', split_axis=1, concat_axis=2, tiled=True)  26.7 us
    all_to_all x1, waiting for transfers between devices, body(): lax.all_to_all(query_local, 'seq', split_axis=1, concat_axis=2, tiled=True)  24.9 us
  transfers between devices with their start and end apart: 5, of which 4 were waited for; matrix products, arithmetic and copies ran while one was open for 12% of the time, Pallas kernels for 0%

commit v1 on v0

v1 whole, which is shorter than its diff:
```python
import functools
import math

import jax
import jax.numpy as jnp
from jax import lax
from jax.experimental import pallas as pl
from jax.experimental.pallas import tpu as pltpu
from jax.sharding import PartitionSpec as P

EPSILON = 1e-06
HEADS = 40
HDIM = 128
SEQ = 16
CHUNKS = 4
GROUP = 16
MESH = pl.DeviceIdType.MESH
NEGATIVE = -1e30


def peer_of(me, step):
    x = lax.rem(lax.div(me, 8) + lax.div(step, 8), 2)
    z = lax.rem(lax.div(me, 2) + lax.div(step, 2), 4)
    core = lax.rem(me + step, 2)
    return x * 8 + z * 2 + core


def kernel(
    dp_size,
    q_hbm, k_hbm, v_hbm, g_hbm, qgain_ref, kgain_ref,
    oq, ok, ov, oqg, okg,
    raw, nrm, rcv, stg, ret, mask, gsend, gbuf, gain, acc, rsend, rbuf, asend, abuf,
    raw_sem, fwd_send, fwd_recv, ret_send, ret_recv, val_send, val_recv, out_sem,
    gain_send, gain_recv, rs_send, rs_recv, ag_send, ag_recv,
):
    me = lax.axis_index("seq")
    dp = lax.axis_index("dp")
    rows = q_hbm.shape[1]
    part = rows // CHUNKS
    local_heads = HEADS // dp_size
    pad = gsend.shape[0] // 2
    scaling = 1.0 / math.sqrt(HDIM)

    def remote(src, dst, send, recv, seq):
        return pltpu.make_async_remote_copy(
            src_ref=src, dst_ref=dst, send_sem=send, recv_sem=recv,
            device_id={"seq": seq}, device_id_type=MESH,
        )

    def remote_dp(src, dst, send, recv, other):
        return pltpu.make_async_remote_copy(
            src_ref=src, dst_ref=dst, send_sem=send, recv_sem=recv,
            device_id={"dp": other}, device_id_type=MESH,
        )

    for a, source in enumerate((q_hbm, k_hbm)):
        pltpu.make_async_copy(source, raw.at[a], raw_sem.at[a]).start()
    gsend[...] = jnp.zeros_like(gsend)
    gsend[0:local_heads] = qgain_ref[...]
    gsend[pad : pad + local_heads] = kgain_ref[...]

    barrier = pltpu.get_barrier_semaphore()
    for step in range(1, SEQ):
        pl.semaphore_signal(
            barrier, inc=1, device_id={"seq": lax.rem(me + step, SEQ)}, device_id_type=MESH
        )
    for step in range(1, dp_size):
        pl.semaphore_signal(
            barrier, inc=1, device_id={"dp": lax.rem(dp + step, dp_size)}, device_id_type=MESH
        )
    pl.semaphore_wait(barrier, SEQ - 1 + dp_size - 1)

    for step in range(1, dp_size):
        remote_dp(
            gsend, gbuf.at[dp], gain_send, gain_recv, lax.rem(dp + step, dp_size)
        ).start()
    pltpu.make_async_copy(gsend, gbuf.at[dp], gain_recv).start()

    def send_values(c):
        here = pl.ds(c * part, part)

        def one(step, carry):
            seq = peer_of(me, step)
            for a, source in ((2, v_hbm), (3, g_hbm)):
                remote(
                    source.at[seq, here], rcv.at[a, c, me], fwd_send.at[a], fwd_recv.at[a, c], seq
                ).start()
            return carry

        lax.fori_loop(1, SEQ, one, 0)
        for a, source in ((2, v_hbm), (3, g_hbm)):
            pltpu.make_async_copy(source.at[me, here], rcv.at[a, c, me], fwd_recv.at[a, c]).start()

    def normalized(a, seq, here):
        wide = raw[a, seq, here].astype(jnp.float32)
        inverse = lax.rsqrt(jnp.mean(wide * wide, axis=-1, keepdims=True) + EPSILON)
        return wide * inverse, inverse

    def by_head(tile, factor):
        split = tile.reshape(part // HEADS, HEADS, HDIM)
        return (split * factor[None]).reshape(part, HDIM)

    def send_normalized(c):
        here = pl.ds(c * part, part)

        def one(step, carry):
            seq = peer_of(me, step)
            for a in range(2):
                hat, _ = normalized(a, seq, here)
                nrm[a, seq, here] = by_head(hat, gain[a]).astype(jnp.bfloat16)

            @pl.when(step > 0)
            def _():
                for a in range(2):
                    remote(
                        nrm.at[a, seq, here], rcv.at[a, c, me],
                        fwd_send.at[a], fwd_recv.at[a, c], seq,
                    ).start()

            @pl.when(step == 0)
            def _():
                for a in range(2):
                    pltpu.make_async_copy(
                        nrm.at[a, me, here], rcv.at[a, c, me], fwd_recv.at[a, c]
                    ).start()

            return carry

        lax.fori_loop(0, SEQ, one, 0)

    send_values(0)
    row_ids = lax.broadcasted_iota(jnp.int32, mask.shape, 0)
    col_ids = lax.broadcasted_iota(jnp.int32, mask.shape, 1)
    allowed = (lax.rem(row_ids, GROUP) == lax.rem(col_ids, GROUP)) & (col_ids <= row_ids)
    mask[...] = jnp.where(allowed, 0.0, NEGATIVE)
    acc[...] = jnp.zeros_like(acc)

    pltpu.make_async_copy(gbuf, gbuf, gain_recv).wait()
    for d in range(dp_size):
        for a in range(2):
            gain[a, d * local_heads : (d + 1) * local_heads] = gbuf[
                d, a * pad : a * pad + local_heads
            ]
    for a, source in enumerate((q_hbm, k_hbm)):
        pltpu.make_async_copy(source, raw.at[a], raw_sem.at[a]).wait()

    send_normalized(0)
    for c in range(1, CHUNKS):
        send_values(c)
        send_normalized(c)

    def contract(left, right, dims):
        return lax.dot_general(left, right, (dims, ((), ())), preferred_element_type=jnp.float32)

    def attention(c):
        for a in range(4):
            pltpu.make_async_copy(rcv.at[a, c], rcv.at[a, c], fwd_recv.at[a, c]).wait()

        def block(b, carry):
            here = pl.ds(pl.multiple_of(b * GROUP, GROUP), GROUP)
            wide = SEQ * GROUP
            query, key, value, grad = (
                rcv[a, c, :, here, :].reshape(wide, HDIM) for a in range(4)
            )
            scores = contract(query, key, ((1,), (1,))) * scaling + mask[...]
            expo = jnp.exp(scores - jnp.max(scores, axis=-1, keepdims=True))
            probability = expo / jnp.sum(expo, axis=-1, keepdims=True)
            prob_low = probability.astype(jnp.bfloat16)
            prob_grad = contract(grad, value, ((1,), (1,)))
            row_dots = jnp.sum(prob_low.astype(jnp.float32) * prob_grad, axis=-1, keepdims=True)
            score_low = (probability * (prob_grad - row_dots)).astype(jnp.bfloat16)
            results = (
                contract(score_low, key, ((1,), (0,))) * scaling,
                contract(score_low, query, ((0,), (0,))) * scaling,
                contract(prob_low, grad, ((0,), (0,))),
            )
            for a, result in enumerate(results):
                stg[a, c, :, here, :] = result.astype(jnp.bfloat16).reshape(SEQ, GROUP, HDIM)
            return carry

        lax.fori_loop(0, part // GROUP, block, 0)

    def send_steps(c):
        def one(step, carry):
            seq = peer_of(me, step)
            for a in range(2):
                remote(
                    stg.at[a, c, seq], ret.at[a, c, me], ret_send.at[a], ret_recv.at[a, c], seq
                ).start()
            return carry

        lax.fori_loop(1, SEQ, one, 0)
        for a in range(2):
            pltpu.make_async_copy(stg.at[a, c, me], ret.at[a, c, me], ret_recv.at[a, c]).start()

    def send_value_grads(c):
        here = pl.ds(c * part, part)

        def one(step, carry):
            seq = peer_of(me, step)
            remote(stg.at[2, c, seq], ov.at[me, here], val_send, val_recv, seq).start()
            return carry

        lax.fori_loop(1, SEQ, one, 0)
        pltpu.make_async_copy(stg.at[2, c, me], ov.at[me, here], val_recv).start()

    def norm_back(c):
        here = pl.ds(c * part, part)
        for a in range(2):
            pltpu.make_async_copy(ret.at[a, c], ret.at[a, c], ret_recv.at[a, c]).wait()

        def one(seq, carry):
            for a in range(2):
                hat, inverse = normalized(a, seq, here)
                step = ret[a, c, seq].astype(jnp.float32)
                gained = by_head(step, gain[a])
                mean = jnp.mean(gained * hat, axis=-1, keepdims=True)
                raw[a, seq, here] = (inverse * (gained - hat * mean)).astype(jnp.bfloat16)
                acc[a] += jnp.sum((step * hat).reshape(part // HEADS, HEADS, HDIM), axis=0)
            return carry

        lax.fori_loop(0, SEQ, one, 0)
        for a, out in enumerate((oq, ok)):
            pltpu.make_async_copy(raw.at[a, :, here], out.at[:, here], out_sem.at[a]).start()

    for c in range(CHUNKS):
        attention(c)
        send_steps(c)
    for c in range(CHUNKS):
        send_value_grads(c)
    for c in range(CHUNKS):
        norm_back(c)

    rsend[...] = jnp.zeros_like(rsend)
    for d in range(dp_size):
        for a in range(2):
            rsend[d, a * pad : a * pad + local_heads] = acc[
                a, d * local_heads : (d + 1) * local_heads
            ]
    for step in range(1, dp_size):
        other = lax.rem(dp + step, dp_size)
        remote_dp(rsend.at[other], rbuf.at[dp], rs_send, rs_recv, other).start()
    pltpu.make_async_copy(rsend.at[dp], rbuf.at[dp], rs_recv).start()
    pltpu.make_async_copy(rbuf, rbuf, rs_recv).wait()
    asend[...] = jnp.sum(rbuf[...], axis=0)
    for step in range(1, SEQ):
        seq = lax.rem(me + step, SEQ)
        remote(asend, abuf.at[me], ag_send, ag_recv, seq).start()
    pltpu.make_async_copy(asend, abuf.at[me], ag_recv).start()
    pltpu.make_async_copy(abuf, abuf, ag_recv).wait()
    total = jnp.sum(abuf[...], axis=0)
    oqg[...] = total[0:local_heads]
    okg[...] = total[pad : pad + local_heads]

    others = pl.ds(0, SEQ - 1)
    pltpu.make_async_copy(ov, ov, val_recv).wait()
    for a, out in enumerate((oq, ok)):
        pltpu.make_async_copy(out, out, out_sem.at[a]).wait()
    for a in range(4):
        pltpu.make_async_copy(oq.at[others], oq.at[others], fwd_send.at[a]).wait()
    for a in range(2):
        pltpu.make_async_copy(oq.at[others], oq.at[others], ret_send.at[a]).wait()
    pltpu.make_async_copy(oq.at[others], oq.at[others], val_send).wait()
    if dp_size > 1:
        most = pl.ds(0, dp_size - 1)
        pltpu.make_async_copy(gbuf.at[most], gbuf.at[most], gain_send).wait()
        pltpu.make_async_copy(rbuf.at[most], rbuf.at[most], rs_send).wait()
    pltpu.make_async_copy(abuf.at[others], abuf.at[others], ag_send).wait()


def body(dp_size, queries, key_proj, value_proj, out_grad, query_gain, key_gain):
    shape = queries.shape
    rows = shape[2] * HEADS // SEQ
    part = rows // CHUNKS
    local_heads = query_gain.shape[0]
    pad = -(-local_heads // 8) * 8
    flat = [v.reshape(SEQ, rows, HDIM) for v in (queries, key_proj, value_proj, out_grad)]
    low, wide = jnp.bfloat16, jnp.float32
    anywhere = pl.BlockSpec(memory_space=pl.ANY)
    vmem = pl.BlockSpec(memory_space=pltpu.VMEM)
    dma = pltpu.SemaphoreType.DMA
    big = jax.ShapeDtypeStruct((SEQ, rows, HDIM), low)
    small = jax.ShapeDtypeStruct((local_heads, HDIM), wide)
    query_grad, key_grad, value_grad, query_total, key_total = pl.pallas_call(
        functools.partial(kernel, dp_size),
        out_shape=(big, big, big, small, small),
        in_specs=[anywhere] * 4 + [vmem] * 2,
        out_specs=(anywhere, anywhere, anywhere, vmem, vmem),
        scratch_shapes=[
            pltpu.VMEM((2, SEQ, rows, HDIM), low),
            pltpu.VMEM((2, SEQ, rows, HDIM), low),
            pltpu.VMEM((4, CHUNKS, SEQ, part, HDIM), low),
            pltpu.VMEM((3, CHUNKS, SEQ, part, HDIM), low),
            pltpu.VMEM((2, CHUNKS, SEQ, part, HDIM), low),
            pltpu.VMEM((SEQ * GROUP, SEQ * GROUP), wide),
            pltpu.VMEM((2 * pad, HDIM), wide),
            pltpu.VMEM((dp_size, 2 * pad, HDIM), wide),
            pltpu.VMEM((2, HEADS, HDIM), wide),
            pltpu.VMEM((2, HEADS, HDIM), wide),
            pltpu.VMEM((dp_size, 2 * pad, HDIM), wide),
            pltpu.VMEM((dp_size, 2 * pad, HDIM), wide),
            pltpu.VMEM((2 * pad, HDIM), wide),
            pltpu.VMEM((SEQ, 2 * pad, HDIM), wide),
            dma((2,)),
            dma((4,)),
            dma((4, CHUNKS)),
            dma((2,)),
            dma((2, CHUNKS)),
            dma,
            dma,
            dma((2,)),
            dma,
            dma,
            dma,
            dma,
            dma,
            dma,
        ],
        compiler_params=pltpu.CompilerParams(
            collective_id=0, has_side_effects=True, vmem_limit_bytes=52 * 2**20
        ),
        name="temporal_attention_backward",
    )(*flat, query_gain, key_gain)
    return (
        query_grad.reshape(shape),
        key_grad.reshape(shape),
        value_grad.reshape(shape),
        query_total,
        key_total,
    )


def solution(mesh):
    blocks = P("dp", "seq", None, None, None)
    gains = P("dp", None)
    return jax.shard_map(
        functools.partial(body, mesh.shape["dp"]),
        mesh=mesh,
        in_specs=(blocks, blocks, blocks, blocks, gains, gains),
        out_specs=(blocks, blocks, blocks, gains, gains),
        check_vma=False,
    )
```

time: 458 us -> 230 us (0.50)
  blocking collectives: 240 us -> 0 us
  Pallas kernels: 0 us -> 219 us
  waiting for transfers between devices: 83.9 us -> 0 us
  starting transfers between devices: 44.8 us -> 0 us
  other arithmetic: 43.1 us -> 0 us
  matrix products: 33.3 us -> 0 us
    pallas_call x0 -> x1, Pallas kernels: none -> 219 us  [body(): pl.pallas_call(functools.partial(kernel, dp_size), out_shape=(big, big, b...]
    all_gather x2 -> x0, blocking collectives: 87.7 us -> none  [the longest x1 58.7 us: body(): lax.all_gather(query_gain, 'dp', axis=0, tiled=True)]
    all_to_all x5 -> x0, waiting for transfers between devices: 83.9 us -> none  [the longest x1 26.7 us: body(): lax.all_to_all(key_local, 'seq', split_axis=1, concat_axis=2, tiled=True)]
    all_to_all x2 -> x0, blocking collectives: 82 us -> none  [the longest x1 44.2 us: body(): lax.all_to_all(query_norm, 'seq', split_axis=2, concat_axis=1, tiled=True)]
    all_to_all x5 -> x0, starting transfers between devices: 44.8 us -> none  [the longest x1 13.3 us: body(): lax.all_to_all(key_norm, 'seq', split_axis=2, concat_axis=1, tiled=True)]
    psum x1 -> x0, blocking collectives: 37.8 us -> none  [body(): totals = lax.psum((query_part, key_part), 'seq')]
    dot_general x6 -> x0, matrix products: 33.3 us -> none  [the longest x1 10.9 us: attention_grads(): jnp.einsum('ephfg,egphd->efphd', prob_low, value_in, preferred_element_ty...]
    unnamed x1 -> x0, blocking collectives: 32.2 us -> none
  transfers between devices with their start and end apart: 5 -> 0, of which waited for: 4 -> 0; matrix products, arithmetic and copies ran while one was open for 12% -> 0% of each run, Pallas kernels for 0% -> 0%
where the time goes in v1:
time: 230 us
  Pallas kernels  219 us (95%)
  local copies, waits for them, and re-layouts  10.6 us (5%)
    pallas_call x1, Pallas kernels, body(): pl.pallas_call(functools.partial(kernel, dp_size), out_shape=(big, big, b...  219 us
    unnamed x13, local copies, waits for them, and re-layouts  10.6 us

profile of v1, /device:TPU:1, one launch (start us, length us, event | category | flops | bytes accessed | tf_op | source)
XLA Modules:
  0.0 229.8 jit_solution(4894341988509403979)
XLA Ops:
  0.6 0.0 copy-start
  0.6 0.7 copy-done
  1.3 0.0 copy-start.1
  1.3 0.7 copy-done.1
  2.0 218.6 %temporal_attention_backward.1 = (bf16[16,640,128]{2,1,0:T(8,128)(2,1)}, bf16[16,640,128]{2,1,0:T(8,128)(2,1)}, bf16[16,640,128]{2,1,0:T(8,128)(2,1)}, f32[5,128]{1,0:T(8,128)S(1)}, f32[5,128]{1,0:T(8,128)S(1)}) custom-call(bf16[16,640,128]{2,1,0:T(8,128)(2,1)} %bitcast.10, bf16[16,640,128]{2,1,0:T(8,128)(2,1)} %bitcast.11, bf16[16,640,128]{2,1,0:T(8,128)(2,1)} %bitcast.12, ...), custom_call_target="tpu_custom_call" | custom-call | tf_op jit(solution)/shard_map/temporal_attention_backward/pallas_call | solution.py:284
  220.6 0.0 copy-start.3
  220.6 3.8 %copy.16 = bf16[1,1,256,40,128]{4,3,2,1,0:T(8,128)(2,1)} copy(bf16[1,1,256,40,128]{4,3,2,1,0:T(8,128)(2,1)} %bitcast.9) | data formatting | bytes 5242880
  224.5 0.0 copy-done.3
  224.5 0.0 copy-start.2
  224.5 1.5 copy.17
  226.0 1.2 copy-done.2
  227.2 1.5 copy.18
  228.6 0.6 copy.19
  229.2 0.6 copy.20
Async XLA Ops:
  0.6 0.7 copy-start
  1.3 0.7 copy-start.1
  220.6 3.8 %copy-start.3 = (bf16[16,640,128]{2,1,0:T(8,128)(2,1)S(1)}, bf16[16,640,128]{2,1,0:T(8,128)(2,1)}, u32[]{:S(2)}) copy-start(bf16[16,640,128]{2,1,0:T(8,128)(2,1)} %get-tuple-element.11) | copy-start | bytes 7864324
  224.5 2.7 %copy-start.2 = (bf16[16,640,128]{2,1,0:T(8,128)(2,1)S(1)}, bf16[16,640,128]{2,1,0:T(8,128)(2,1)}, u32[]{:S(2)}) copy-start(bf16[16,640,128]{2,1,0:T(8,128)(2,1)} %get-tuple-element.12) | copy-start | bytes 7864324

commit v2 on v1

--- a/solution.py
+++ b/solution.py
@@ -12,13 +12,14 @@
 HEADS = 40
 HDIM = 128
 SEQ = 16
-CHUNKS = 4
+CHUNKS = 8
 GROUP = 16
 MESH = pl.DeviceIdType.MESH
 NEGATIVE = -1e30
 
 
 def peer_of(me, step):
+    step = lax.rem(step * 9, SEQ)
     x = lax.rem(lax.div(me, 8) + lax.div(step, 8), 2)
     z = lax.rem(lax.div(me, 2) + lax.div(step, 2), 4)
     core = lax.rem(me + step, 2)
@@ -27,10 +28,10 @@
 
 def kernel(
     dp_size,
-    q_hbm, k_hbm, v_hbm, g_hbm, qgain_ref, kgain_ref,
-    oq, ok, ov, oqg, okg,
-    raw, nrm, rcv, stg, ret, mask, gsend, gbuf, gain, acc, rsend, rbuf, asend, abuf,
-    raw_sem, fwd_send, fwd_recv, ret_send, ret_recv, val_send, val_recv, out_sem,
+    q_hbm, k_hbm, v_hbm, g_hbm, qgain_hbm, kgain_hbm,
+    oq, ok, ov, total_gain,
+    nrm, rcv, stg, ret, mask, gsend, gbuf, gain, acc, rsend, rbuf, asend, abuf,
+    raw_sem, load_sem, fwd_send, fwd_recv, ret_send, ret_recv, val_send, val_recv,
     gain_send, gain_recv, rs_send, rs_recv, ag_send, ag_recv,
 ):
     me = lax.axis_index("seq")
@@ -53,11 +54,18 @@
             device_id={"dp": other}, device_id_type=MESH,
         )
 
-    for a, source in enumerate((q_hbm, k_hbm)):
-        pltpu.make_async_copy(source, raw.at[a], raw_sem.at[a]).start()
+    held = (oq, ok)
     gsend[...] = jnp.zeros_like(gsend)
-    gsend[0:local_heads] = qgain_ref[...]
-    gsend[pad : pad + local_heads] = kgain_ref[...]
+    gain_loads = [
+        pltpu.make_async_copy(source, gsend.at[pl.ds(a * pad, local_heads)], load_sem.at[a])
+        for a, source in enumerate((qgain_hbm, kgain_hbm))
+    ]
+    raw_loads = [
+        pltpu.make_async_copy(source, held[a], raw_sem.at[a])
+        for a, source in enumerate((q_hbm, k_hbm))
+    ]
+    for copy in gain_loads + raw_loads:
+        copy.start()
 
     barrier = pltpu.get_barrier_semaphore()
     for step in range(1, SEQ):
@@ -70,6 +78,8 @@
         )
     pl.semaphore_wait(barrier, SEQ - 1 + dp_size - 1)
 
+    for copy in gain_loads:
+        copy.wait()
     for step in range(1, dp_size):
         remote_dp(
             gsend, gbuf.at[dp], gain_send, gain_recv, lax.rem(dp + step, dp_size)
@@ -92,7 +102,7 @@
             pltpu.make_async_copy(source.at[me, here], rcv.at[a, c, me], fwd_recv.at[a, c]).start()
 
     def normalized(a, seq, here):
-        wide = raw[a, seq, here].astype(jnp.float32)
+        wide = held[a][seq, here].astype(jnp.float32)
         inverse = lax.rsqrt(jnp.mean(wide * wide, axis=-1, keepdims=True) + EPSILON)
         return wide * inverse, inverse
 
@@ -141,8 +151,8 @@
             gain[a, d * local_heads : (d + 1) * local_heads] = gbuf[
                 d, a * pad : a * pad + local_heads
             ]
-    for a, source in enumerate((q_hbm, k_hbm)):
-        pltpu.make_async_copy(source, raw.at[a], raw_sem.at[a]).wait()
+    for copy in raw_loads:
+        copy.wait()
 
     send_normalized(0)
     for c in range(1, CHUNKS):
@@ -215,19 +225,22 @@
                 step = ret[a, c, seq].astype(jnp.float32)
                 gained = by_head(step, gain[a])
                 mean = jnp.mean(gained * hat, axis=-1, keepdims=True)
-                raw[a, seq, here] = (inverse * (gained - hat * mean)).astype(jnp.bfloat16)
+                held[a][seq, here] = (inverse * (gained - hat * mean)).astype(jnp.bfloat16)
                 acc[a] += jnp.sum((step * hat).reshape(part // HEADS, HEADS, HDIM), axis=0)
             return carry
 
         lax.fori_loop(0, SEQ, one, 0)
-        for a, out in enumerate((oq, ok)):
-            pltpu.make_async_copy(raw.at[a, :, here], out.at[:, here], out_sem.at[a]).start()
+
+    lots = (0, CHUNKS // 4, CHUNKS // 2, CHUNKS)
+
+    def send_lot(lot):
+        for c in range(lots[lot], lots[lot + 1]):
+            send_value_grads(c)
 
     for c in range(CHUNKS):
         attention(c)
         send_steps(c)
-    for c in range(CHUNKS):
-        send_value_grads(c)
+    send_lot(0)
     for c in range(CHUNKS):
         norm_back(c)
 
@@ -241,21 +254,19 @@
         other = lax.rem(dp + step, dp_size)
         remote_dp(rsend.at[other], rbuf.at[dp], rs_send, rs_recv, other).start()
     pltpu.make_async_copy(rsend.at[dp], rbuf.at[dp], rs_recv).start()
+    send_lot(1)
     pltpu.make_async_copy(rbuf, rbuf, rs_recv).wait()
     asend[...] = jnp.sum(rbuf[...], axis=0)
     for step in range(1, SEQ):
         seq = lax.rem(me + step, SEQ)
         remote(asend, abuf.at[me], ag_send, ag_recv, seq).start()
     pltpu.make_async_copy(asend, abuf.at[me], ag_recv).start()
+    send_lot(2)
     pltpu.make_async_copy(abuf, abuf, ag_recv).wait()
-    total = jnp.sum(abuf[...], axis=0)
-    oqg[...] = total[0:local_heads]
-    okg[...] = total[pad : pad + local_heads]
+    total_gain[...] = jnp.sum(abuf[...], axis=0)
 
     others = pl.ds(0, SEQ - 1)
     pltpu.make_async_copy(ov, ov, val_recv).wait()
-    for a, out in enumerate((oq, ok)):
-        pltpu.make_async_copy(out, out, out_sem.at[a]).wait()
     for a in range(4):
         pltpu.make_async_copy(oq.at[others], oq.at[others], fwd_send.at[a]).wait()
     for a in range(2):
@@ -266,6 +277,22 @@
         pltpu.make_async_copy(gbuf.at[most], gbuf.at[most], gain_send).wait()
         pltpu.make_async_copy(rbuf.at[most], rbuf.at[most], rs_send).wait()
     pltpu.make_async_copy(abuf.at[others], abuf.at[others], ag_send).wait()
+
+
+def write_out(local_heads, oq, ok, ov, total_gain, *refs):
+    outs, sems = refs[:5], refs[5]
+    pad = total_gain.shape[0] // 2
+    sources = (
+        oq, ok, ov, total_gain.at[pl.ds(0, local_heads)], total_gain.at[pl.ds(pad, local_heads)]
+    )
+    copies = [
+        pltpu.make_async_copy(source, out, sems.at[i])
+        for i, (source, out) in enumerate(zip(sources, outs))
+    ]
+    for copy in copies:
+        copy.start()
+    for copy in copies:
+        copy.wait()
 
 
 def body(dp_size, queries, key_proj, value_proj, out_grad, query_gain, key_gain):
@@ -281,13 +308,12 @@
     dma = pltpu.SemaphoreType.DMA
     big = jax.ShapeDtypeStruct((SEQ, rows, HDIM), low)
     small = jax.ShapeDtypeStruct((local_heads, HDIM), wide)
-    query_grad, key_grad, value_grad, query_total, key_total = pl.pallas_call(
+    results = pl.pallas_call(
         functools.partial(kernel, dp_size),
-        out_shape=(big, big, big, small, small),
-        in_specs=[anywhere] * 4 + [vmem] * 2,
-        out_specs=(anywhere, anywhere, anywhere, vmem, vmem),
+        out_shape=(big, big, big, jax.ShapeDtypeStruct((2 * pad, HDIM), wide)),
+        in_specs=[anywhere] * 6,
+        out_specs=(vmem,) * 4,
         scratch_shapes=[
-            pltpu.VMEM((2, SEQ, rows, HDIM), low),
             pltpu.VMEM((2, SEQ, rows, HDIM), low),
             pltpu.VMEM((4, CHUNKS, SEQ, part, HDIM), low),
             pltpu.VMEM((3, CHUNKS, SEQ, part, HDIM), low),
@@ -302,13 +328,13 @@
             pltpu.VMEM((2 * pad, HDIM), wide),
             pltpu.VMEM((SEQ, 2 * pad, HDIM), wide),
             dma((2,)),
+            dma((2,)),
             dma((4,)),
             dma((4, CHUNKS)),
             dma((2,)),
             dma((2, CHUNKS)),
             dma,
             dma,
-            dma((2,)),
             dma,
             dma,
             dma,
@@ -317,10 +343,19 @@
             dma,
         ],
         compiler_params=pltpu.CompilerParams(
-            collective_id=0, has_side_effects=True, vmem_limit_bytes=52 * 2**20
+            collective_id=0, has_side_effects=True, vmem_limit_bytes=44 * 2**20
         ),
         name="temporal_attention_backward",
     )(*flat, query_gain, key_gain)
+    query_grad, key_grad, value_grad, query_total, key_total = pl.pallas_call(
+        functools.partial(write_out, local_heads),
+        out_shape=(big, big, big, small, small),
+        in_specs=[vmem] * 4,
+        out_specs=(anywhere,) * 5,
+        scratch_shapes=[dma((5,))],
+        compiler_params=pltpu.CompilerParams(vmem_limit_bytes=2**20),
+        name="write_out",
+    )(*results)
     return (
         query_grad.reshape(shape),
         key_grad.reshape(shape),

time: 230 us -> 216 us (0.939)
  local copies, waits for them, and re-layouts: 10.6 us -> 1.37 us
  Pallas kernels: 219 us -> 213 us
    unnamed x13 -> x4, local copies, waits for them, and re-layouts: 10.6 us -> 1.37 us
    pallas_call x1, Pallas kernels: 219 us -> 210 us  [body(): pl.pallas_call(functools.partial(kernel, dp_size), out_shape=(big, big, b...]
    pallas_call x0 -> x1, Pallas kernels: none -> 3.27 us  [body(): pl.pallas_call(functools.partial(write_out, local_heads), out_shape=(big,...]
where the time goes in v2:
time: 216 us; the launch traced here: 215 us
  Pallas kernels  213 us (99%)
    pallas_call x1, Pallas kernels, body(): pl.pallas_call(functools.partial(kernel, dp_size), out_shape=(big, big, b...  210 us

profile of v2, /device:TPU:1, one launch (start us, length us, event | category | flops | bytes accessed | tf_op | source)
XLA Modules:
  0.0 215.3 jit_solution(2555104906281851075)
XLA Ops:
  0.6 0.0 copy-start
  0.6 0.7 copy-done
  1.3 0.0 copy-start.1
  1.3 0.7 copy-done.1
  2.0 210.0 %temporal_attention_backward.1 = (bf16[16,640,128]{2,1,0:T(8,128)(2,1)S(1)}, bf16[16,640,128]{2,1,0:T(8,128)(2,1)S(1)}, bf16[16,640,128]{2,1,0:T(8,128)(2,1)S(1)}, f32[16,128]{1,0:T(8,128)S(1)}) custom-call(bf16[16,640,128]{2,1,0:T(8,128)(2,1)} %bitcast.7, bf16[16,640,128]{2,1,0:T(8,128)(2,1)} %bitcast.8, bf16[16,640,128]{2,1,0:T(8,128)(2,1)} %bitcast.9, ...), custom_call_target="tpu_custom_call" | custom-call | tf_op jit(solution)/shard_map/temporal_attention_backward/pallas_call | solution.py:311
  212.0 3.3 %write_out.1 = (bf16[16,640,128]{2,1,0:T(8,128)(2,1)}, bf16[16,640,128]{2,1,0:T(8,128)(2,1)}, bf16[16,640,128]{2,1,0:T(8,128)(2,1)}, f32[5,128]{1,0:T(8,128)}, f32[5,128]{1,0:T(8,128)}) custom-call(bf16[16,640,128]{2,1,0:T(8,128)(2,1)S(1)} %get-tuple-element.14.oq, bf16[16,640,128]{2,1,0:T(8,128)(2,1)S(1)} %get-tuple-element.15.ok, ...), custom_call_target="tpu_custom_call" | custom-call | tf_op jit(solution)/shard_map/write_out/pallas_call | solution.py:350
Async XLA Ops:
  0.6 0.7 copy-start
  1.3 0.7 copy-start.1

commit v3 on v2

--- a/solution.py
+++ b/solution.py
@@ -30,16 +30,16 @@
     dp_size,
     q_hbm, k_hbm, v_hbm, g_hbm, qgain_hbm, kgain_hbm,
     oq, ok, ov, total_gain,
-    nrm, rcv, stg, ret, mask, gsend, gbuf, gain, acc, rsend, rbuf, asend, abuf,
+    nrm, rcv, stg, ret, mask, gsend, gbuf, gain, acc, rsend, rbuf, asend, abuf, row, bbuf,
     raw_sem, load_sem, fwd_send, fwd_recv, ret_send, ret_recv, val_send, val_recv,
-    gain_send, gain_recv, rs_send, rs_recv, ag_send, ag_recv,
+    gain_send, gain_recv, rs_send, rs_recv, row_send, row_recv, ag_send, ag_recv,
 ):
     me = lax.axis_index("seq")
     dp = lax.axis_index("dp")
     rows = q_hbm.shape[1]
     part = rows // CHUNKS
     local_heads = HEADS // dp_size
-    pad = gsend.shape[0] // 2
+    pad = SEQ // 2
     scaling = 1.0 / math.sqrt(HDIM)
 
     def remote(src, dst, send, recv, seq):
@@ -231,7 +231,7 @@
 
         lax.fori_loop(0, SEQ, one, 0)
 
-    lots = (0, CHUNKS // 4, CHUNKS // 2, CHUNKS)
+    lots = (0, CHUNKS // 4, CHUNKS // 2, 3 * CHUNKS // 4, CHUNKS)
 
     def send_lot(lot):
         for c in range(lots[lot], lots[lot + 1]):
@@ -256,14 +256,21 @@
     pltpu.make_async_copy(rsend.at[dp], rbuf.at[dp], rs_recv).start()
     send_lot(1)
     pltpu.make_async_copy(rbuf, rbuf, rs_recv).wait()
-    asend[...] = jnp.sum(rbuf[...], axis=0)
+    asend[...] = jnp.sum(rbuf[...], axis=0).reshape(asend.shape)
     for step in range(1, SEQ):
         seq = lax.rem(me + step, SEQ)
-        remote(asend, abuf.at[me], ag_send, ag_recv, seq).start()
-    pltpu.make_async_copy(asend, abuf.at[me], ag_recv).start()
+        remote(asend.at[seq], abuf.at[me], row_send, row_recv, seq).start()
+    pltpu.make_async_copy(asend.at[me], abuf.at[me], row_recv).start()
     send_lot(2)
-    pltpu.make_async_copy(abuf, abuf, ag_recv).wait()
-    total_gain[...] = jnp.sum(abuf[...], axis=0)
+    pltpu.make_async_copy(abuf, abuf, row_recv).wait()
+    row[...] = jnp.sum(abuf[...], axis=0)
+    for step in range(1, SEQ):
+        seq = lax.rem(me + step, SEQ)
+        remote(row, bbuf.at[me], ag_send, ag_recv, seq).start()
+    pltpu.make_async_copy(row, bbuf.at[me], ag_recv).start()
+    send_lot(3)
+    pltpu.make_async_copy(bbuf, bbuf, ag_recv).wait()
+    total_gain[...] = bbuf[...].reshape(total_gain.shape)
 
     others = pl.ds(0, SEQ - 1)
     pltpu.make_async_copy(ov, ov, val_recv).wait()
@@ -276,19 +283,22 @@
         most = pl.ds(0, dp_size - 1)
         pltpu.make_async_copy(gbuf.at[most], gbuf.at[most], gain_send).wait()
         pltpu.make_async_copy(rbuf.at[most], rbuf.at[most], rs_send).wait()
-    pltpu.make_async_copy(abuf.at[others], abuf.at[others], ag_send).wait()
+    pltpu.make_async_copy(abuf.at[others], abuf.at[others], row_send).wait()
+    pltpu.make_async_copy(bbuf.at[others], bbuf.at[others], ag_send).wait()
 
 
 def write_out(local_heads, oq, ok, ov, total_gain, *refs):
     outs, sems = refs[:5], refs[5]
     pad = total_gain.shape[0] // 2
-    sources = (
-        oq, ok, ov, total_gain.at[pl.ds(0, local_heads)], total_gain.at[pl.ds(pad, local_heads)]
-    )
+    quarter = SEQ // 4
     copies = [
-        pltpu.make_async_copy(source, out, sems.at[i])
-        for i, (source, out) in enumerate(zip(sources, outs))
+        pltpu.make_async_copy(source.at[here], out.at[here], sems.at[i, n])
+        for n, here in enumerate(pl.ds(q * quarter, quarter) for q in range(4))
+        for i, (source, out) in enumerate(zip((oq, ok, ov), outs))
     ]
+    for a in range(2):
+        source = total_gain.at[pl.ds(a * pad, local_heads)]
+        copies.append(pltpu.make_async_copy(source, outs[3 + a], sems.at[3, a]))
     for copy in copies:
         copy.start()
     for copy in copies:
@@ -300,7 +310,7 @@
     rows = shape[2] * HEADS // SEQ
     part = rows // CHUNKS
     local_heads = query_gain.shape[0]
-    pad = -(-local_heads // 8) * 8
+    pad = SEQ // 2
     flat = [v.reshape(SEQ, rows, HDIM) for v in (queries, key_proj, value_proj, out_grad)]
     low, wide = jnp.bfloat16, jnp.float32
     anywhere = pl.BlockSpec(memory_space=pl.ANY)
@@ -325,14 +335,18 @@
             pltpu.VMEM((2, HEADS, HDIM), wide),
             pltpu.VMEM((dp_size, 2 * pad, HDIM), wide),
             pltpu.VMEM((dp_size, 2 * pad, HDIM), wide),
-            pltpu.VMEM((2 * pad, HDIM), wide),
-            pltpu.VMEM((SEQ, 2 * pad, HDIM), wide),
+            pltpu.VMEM((SEQ, 1, HDIM), wide),
+            pltpu.VMEM((SEQ, 1, HDIM), wide),
+            pltpu.VMEM((1, HDIM), wide),
+            pltpu.VMEM((SEQ, 1, HDIM), wide),
             dma((2,)),
             dma((2,)),
             dma((4,)),
             dma((4, CHUNKS)),
             dma((2,)),
             dma((2, CHUNKS)),
+            dma,
+            dma,
             dma,
             dma,
             dma,
@@ -352,7 +366,7 @@
         out_shape=(big, big, big, small, small),
         in_specs=[vmem] * 4,
         out_specs=(anywhere,) * 5,
-        scratch_shapes=[dma((5,))],
+        scratch_shapes=[dma((4, 4))],
         compiler_params=pltpu.CompilerParams(vmem_limit_bytes=2**20),
         name="write_out",
     )(*results)

time: 216 us -> 214 us (level)
  no operation moved by 1% of the time
where the time goes in v3:
time: 214 us
  Pallas kernels  212 us (99%)
    pallas_call x1, Pallas kernels, body(): pl.pallas_call(functools.partial(kernel, dp_size), out_shape=(big, big, b...  209 us

profile of v3, /device:TPU:1, one launch (start us, length us, event | category | flops | bytes accessed | tf_op | source)
XLA Modules:
  0.0 214.1 jit_solution(5939175511253964393)
XLA Ops:
  0.6 0.0 copy-start
  0.6 0.7 copy-done
  1.3 0.0 copy-start.1
  1.3 0.7 copy-done.1
  2.0 208.8 %temporal_attention_backward.1 = (bf16[16,640,128]{2,1,0:T(8,128)(2,1)S(1)}, bf16[16,640,128]{2,1,0:T(8,128)(2,1)S(1)}, bf16[16,640,128]{2,1,0:T(8,128)(2,1)S(1)}, f32[16,128]{1,0:T(8,128)S(1)}) custom-call(bf16[16,640,128]{2,1,0:T(8,128)(2,1)} %bitcast.7, bf16[16,640,128]{2,1,0:T(8,128)(2,1)} %bitcast.8, bf16[16,640,128]{2,1,0:T(8,128)(2,1)} %bitcast.9, ...), custom_call_target="tpu_custom_call" | custom-call | tf_op jit(solution)/shard_map/temporal_attention_backward/pallas_call | solution.py:321
  210.8 3.3 %write_out.1 = (bf16[16,640,128]{2,1,0:T(8,128)(2,1)}, bf16[16,640,128]{2,1,0:T(8,128)(2,1)}, bf16[16,640,128]{2,1,0:T(8,128)(2,1)}, f32[5,128]{1,0:T(8,128)}, f32[5,128]{1,0:T(8,128)}) custom-call(bf16[16,640,128]{2,1,0:T(8,128)(2,1)S(1)} %get-tuple-element.14.oq, bf16[16,640,128]{2,1,0:T(8,128)(2,1)S(1)} %get-tuple-element.15.ok, ...), custom_call_target="tpu_custom_call" | custom-call | tf_op jit(solution)/shard_map/write_out/pallas_call | solution.py:364
Async XLA Ops:
  0.6 0.7 copy-start
  1.3 0.7 copy-start.1

commit v4 on v3

--- a/solution.py
+++ b/solution.py
@@ -28,7 +28,7 @@
 
 def kernel(
     dp_size,
-    q_hbm, k_hbm, v_hbm, g_hbm, qgain_hbm, kgain_hbm,
+    q_hbm, k_hbm, v_hbm, g_hbm, gains_hbm,
     oq, ok, ov, total_gain,
     nrm, rcv, stg, ret, mask, gsend, gbuf, gain, acc, rsend, rbuf, asend, abuf, row, bbuf,
     raw_sem, load_sem, fwd_send, fwd_recv, ret_send, ret_recv, val_send, val_recv,
@@ -54,19 +54,6 @@
             device_id={"dp": other}, device_id_type=MESH,
         )
 
-    held = (oq, ok)
-    gsend[...] = jnp.zeros_like(gsend)
-    gain_loads = [
-        pltpu.make_async_copy(source, gsend.at[pl.ds(a * pad, local_heads)], load_sem.at[a])
-        for a, source in enumerate((qgain_hbm, kgain_hbm))
-    ]
-    raw_loads = [
-        pltpu.make_async_copy(source, held[a], raw_sem.at[a])
-        for a, source in enumerate((q_hbm, k_hbm))
-    ]
-    for copy in gain_loads + raw_loads:
-        copy.start()
-
     barrier = pltpu.get_barrier_semaphore()
     for step in range(1, SEQ):
         pl.semaphore_signal(
@@ -76,6 +63,16 @@
         pl.semaphore_signal(
             barrier, inc=1, device_id={"dp": lax.rem(dp + step, dp_size)}, device_id_type=MESH
         )
+
+    held = (oq, ok)
+    gain_loads = [pltpu.make_async_copy(gains_hbm, gsend, load_sem)]
+    raw_loads = [
+        pltpu.make_async_copy(source, held[a], raw_sem.at[a])
+        for a, source in enumerate((q_hbm, k_hbm))
+    ]
+    for copy in gain_loads + raw_loads:
+        copy.start()
+
     pl.semaphore_wait(barrier, SEQ - 1 + dp_size - 1)
 
     for copy in gain_loads:
@@ -313,6 +310,8 @@
     pad = SEQ // 2
     flat = [v.reshape(SEQ, rows, HDIM) for v in (queries, key_proj, value_proj, out_grad)]
     low, wide = jnp.bfloat16, jnp.float32
+    gap = ((0, pad - local_heads), (0, 0))
+    gains = jnp.concatenate([jnp.pad(query_gain, gap), jnp.pad(key_gain, gap)], axis=0)
     anywhere = pl.BlockSpec(memory_space=pl.ANY)
     vmem = pl.BlockSpec(memory_space=pltpu.VMEM)
     dma = pltpu.SemaphoreType.DMA
@@ -321,7 +320,7 @@
     results = pl.pallas_call(
         functools.partial(kernel, dp_size),
         out_shape=(big, big, big, jax.ShapeDtypeStruct((2 * pad, HDIM), wide)),
-        in_specs=[anywhere] * 6,
+        in_specs=[anywhere] * 5,
         out_specs=(vmem,) * 4,
         scratch_shapes=[
             pltpu.VMEM((2, SEQ, rows, HDIM), low),
@@ -340,7 +339,7 @@
             pltpu.VMEM((1, HDIM), wide),
             pltpu.VMEM((SEQ, 1, HDIM), wide),
             dma((2,)),
-            dma((2,)),
+            dma,
             dma((4,)),
             dma((4, CHUNKS)),
             dma((2,)),
@@ -360,7 +359,7 @@
             collective_id=0, has_side_effects=True, vmem_limit_bytes=44 * 2**20
         ),
         name="temporal_attention_backward",
-    )(*flat, query_gain, key_gain)
+    )(*flat, gains)
     query_grad, key_grad, value_grad, query_total, key_total = pl.pallas_call(
         functools.partial(write_out, local_heads),
         out_shape=(big, big, big, small, small),

time: 214 us -> 214 us (level)
  no operation moved by 1% of the time
where the time goes in v4:
time: 214 us; the launch traced here: 213 us
  Pallas kernels  212 us (99%)
    pallas_call x1, Pallas kernels, body(): pl.pallas_call(functools.partial(kernel, dp_size), out_shape=(big, big, b...  209 us

profile of v4, /device:TPU:1, one launch (start us, length us, event | category | flops | bytes accessed | tf_op | source)
XLA Modules:
  0.0 213.4 jit_solution(9394570279766448842)
XLA Ops:
  0.6 0.7 select_maximum_fusion.gains_hbm
  1.3 208.7 %temporal_attention_backward.1 = (bf16[16,640,128]{2,1,0:T(8,128)(2,1)S(1)}, bf16[16,640,128]{2,1,0:T(8,128)(2,1)S(1)}, bf16[16,640,128]{2,1,0:T(8,128)(2,1)S(1)}, f32[16,128]{1,0:T(8,128)S(1)}) custom-call(bf16[16,640,128]{2,1,0:T(8,128)(2,1)} %bitcast.7, bf16[16,640,128]{2,1,0:T(8,128)(2,1)} %bitcast.8, bf16[16,640,128]{2,1,0:T(8,128)(2,1)} %bitcast.9, ...), custom_call_target="tpu_custom_call" | custom-call | tf_op jit(solution)/shard_map/temporal_attention_backward/pallas_call | solution.py:320
  210.1 3.3 %write_out.1 = (bf16[16,640,128]{2,1,0:T(8,128)(2,1)}, bf16[16,640,128]{2,1,0:T(8,128)(2,1)}, bf16[16,640,128]{2,1,0:T(8,128)(2,1)}, f32[5,128]{1,0:T(8,128)}, f32[5,128]{1,0:T(8,128)}) custom-call(bf16[16,640,128]{2,1,0:T(8,128)(2,1)S(1)} %get-tuple-element.14.oq, bf16[16,640,128]{2,1,0:T(8,128)(2,1)S(1)} %get-tuple-element.15.ok, ...), custom_call_target="tpu_custom_call" | custom-call | tf_op jit(solution)/shard_map/write_out/pallas_call | solution.py:363

commit v5 on v4

--- a/solution.py
+++ b/solution.py
@@ -33,6 +33,7 @@
     nrm, rcv, stg, ret, mask, gsend, gbuf, gain, acc, rsend, rbuf, asend, abuf, row, bbuf,
     raw_sem, load_sem, fwd_send, fwd_recv, ret_send, ret_recv, val_send, val_recv,
     gain_send, gain_recv, rs_send, rs_recv, row_send, row_recv, ag_send, ag_recv,
+    ready, everyone,
 ):
     me = lax.axis_index("seq")
     dp = lax.axis_index("dp")
@@ -59,10 +60,13 @@
         pl.semaphore_signal(
             barrier, inc=1, device_id={"seq": lax.rem(me + step, SEQ)}, device_id_type=MESH
         )
-    for step in range(1, dp_size):
-        pl.semaphore_signal(
-            barrier, inc=1, device_id={"dp": lax.rem(dp + step, dp_size)}, device_id_type=MESH
-        )
+
+    @pl.when(me == 0)
+    def _():
+        for step in range(1, dp_size):
+            pl.semaphore_signal(
+                barrier, inc=1, device_id={"dp": lax.rem(dp + step, dp_size)}, device_id_type=MESH
+            )
 
     held = (oq, ok)
     gain_loads = [pltpu.make_async_copy(gains_hbm, gsend, load_sem)]
@@ -73,7 +77,83 @@
     for copy in gain_loads + raw_loads:
         copy.start()
 
-    pl.semaphore_wait(barrier, SEQ - 1 + dp_size - 1)
+    @pl.when(me == 0)
+    def _():
+        pl.semaphore_wait(barrier, SEQ - 1 + dp_size - 1)
+
+    @pl.when(me > 0)
+    def _():
+        pl.semaphore_wait(barrier, SEQ - 1)
+
+    def send_values(c):
+        here = pl.ds(c * part, part)
+
+        def one(step, carry):
+            seq = peer_of(me, step)
+            for a, source in ((2, v_hbm), (3, g_hbm)):
+                remote(
+                    source.at[seq, here], rcv.at[a, c, me], fwd_send.at[a], fwd_recv.at[a, c], seq
+                ).start()
+            return carry
+
+        lax.fori_loop(1, SEQ, one, 0)
+        for a, source in ((2, v_hbm), (3, g_hbm)):
+            pltpu.make_async_copy(source.at[me, here], rcv.at[a, c, me], fwd_recv.at[a, c]).start()
+
+    def normalized(a, seq, here):
+        wide = held[a][seq, here].astype(jnp.float32)
+        inverse = lax.rsqrt(jnp.mean(wide * wide, axis=-1, keepdims=True) + EPSILON)
+        return wide * inverse, inverse
+
+    def by_head(tile, factor):
+        split = tile.reshape(part // HEADS, HEADS, HDIM)
+        return (split * factor[None]).reshape(part, HDIM)
+
+    def send_normalized(c):
+        here = pl.ds(c * part, part)
+
+        def one(step, carry):
+            seq = peer_of(me, step)
+            for a in range(2):
+                hat, _ = normalized(a, seq, here)
+                nrm[a, seq, here] = by_head(hat, gain[a]).astype(jnp.bfloat16)
+
+            @pl.when(step > 0)
+            def _():
+                for a in range(2):
+                    remote(
+                        nrm.at[a, seq, here], rcv.at[a, c, me],
+                        fwd_send.at[a], fwd_recv.at[a, c], seq,
+                    ).start()
+
+            @pl.when(step == 0)
+            def _():
+                for a in range(2):
+                    pltpu.make_async_copy(
+                        nrm.at[a, me, here], rcv.at[a, c, me], fwd_recv.at[a, c]
+                    ).start()
+
+            return carry
+
+        lax.fori_loop(0, SEQ, one, 0)
+
+    send_values(0)
+
+    @pl.when(me == 0)
+    def _():
+        for step in range(1, dp_size):
+            pl.semaphore_signal(
+                ready, inc=1, device_id={"dp": lax.rem(dp + step, dp_size)}, device_id_type=MESH
+            )
+        pl.semaphore_wait(ready, dp_size - 1)
+        for step in range(1, SEQ):
+            pl.semaphore_signal(
+                everyone, inc=1, device_id={"seq": lax.rem(me + step, SEQ)}, device_id_type=MESH
+            )
+
+    @pl.when(me > 0)
+    def _():
+        pl.semaphore_wait(everyone, 1)
 
     for copy in gain_loads:
         copy.wait()
@@ -82,60 +162,8 @@
             gsend, gbuf.at[dp], gain_send, gain_recv, lax.rem(dp + step, dp_size)
         ).start()
     pltpu.make_async_copy(gsend, gbuf.at[dp], gain_recv).start()
-
-    def send_values(c):
-        here = pl.ds(c * part, part)
-
-        def one(step, carry):
-            seq = peer_of(me, step)
-            for a, source in ((2, v_hbm), (3, g_hbm)):
-                remote(
-                    source.at[seq, here], rcv.at[a, c, me], fwd_send.at[a], fwd_recv.at[a, c], seq
-                ).start()
-            return carry
-
-        lax.fori_loop(1, SEQ, one, 0)
-        for a, source in ((2, v_hbm), (3, g_hbm)):
-            pltpu.make_async_copy(source.at[me, here], rcv.at[a, c, me], fwd_recv.at[a, c]).start()
-
-    def normalized(a, seq, here):
-        wide = held[a][seq, here].astype(jnp.float32)
-        inverse = lax.rsqrt(jnp.mean(wide * wide, axis=-1, keepdims=True) + EPSILON)
-        return wide * inverse, inverse
-
-    def by_head(tile, factor):
-        split = tile.reshape(part // HEADS, HEADS, HDIM)
-        return (split * factor[None]).reshape(part, HDIM)
-
-    def send_normalized(c):
-        here = pl.ds(c * part, part)
-
-        def one(step, carry):
-            seq = peer_of(me, step)
-            for a in range(2):
-                hat, _ = normalized(a, seq, here)
-                nrm[a, seq, here] = by_head(hat, gain[a]).astype(jnp.bfloat16)
-
-            @pl.when(step > 0)
-            def _():
-                for a in range(2):
-                    remote(
-                        nrm.at[a, seq, here], rcv.at[a, c, me],
-                        fwd_send.at[a], fwd_recv.at[a, c], seq,
-                    ).start()
-
-            @pl.when(step == 0)
-            def _():
-                for a in range(2):
-                    pltpu.make_async_copy(
-                        nrm.at[a, me, here], rcv.at[a, c, me], fwd_recv.at[a, c]
-                    ).start()
-
-            return carry
-
-        lax.fori_loop(0, SEQ, one, 0)
-
-    send_values(0)
+    send_values(1)
+
     row_ids = lax.broadcasted_iota(jnp.int32, mask.shape, 0)
     col_ids = lax.broadcasted_iota(jnp.int32, mask.shape, 1)
     allowed = (lax.rem(row_ids, GROUP) == lax.rem(col_ids, GROUP)) & (col_ids <= row_ids)
@@ -152,7 +180,8 @@
         copy.wait()
 
     send_normalized(0)
-    for c in range(1, CHUNKS):
+    send_normalized(1)
+    for c in range(2, CHUNKS):
         send_values(c)
         send_normalized(c)
 
@@ -354,6 +383,8 @@
             dma,
             dma,
             dma,
+            pltpu.SemaphoreType.REGULAR,
+            pltpu.SemaphoreType.REGULAR,
         ],
         compiler_params=pltpu.CompilerParams(
             collective_id=0, has_side_effects=True, vmem_limit_bytes=44 * 2**20

time: 214 us -> 212 us (level)
  no operation moved by 1% of the time
where the time goes in v5:
time: 212 us
  Pallas kernels  211 us (100%)
    pallas_call x1, Pallas kernels, body(): pl.pallas_call(functools.partial(kernel, dp_size), out_shape=(big, big, b...  208 us

profile of v5, /device:TPU:1, one launch (start us, length us, event | category | flops | bytes accessed | tf_op | source)
XLA Modules:
  0.0 212.3 jit_solution(1238918719395197390)
XLA Ops:
  0.6 0.7 select_maximum_fusion.gains_hbm
  1.3 207.7 %temporal_attention_backward.1 = (bf16[16,640,128]{2,1,0:T(8,128)(2,1)S(1)}, bf16[16,640,128]{2,1,0:T(8,128)(2,1)S(1)}, bf16[16,640,128]{2,1,0:T(8,128)(2,1)S(1)}, f32[16,128]{1,0:T(8,128)S(1)}) custom-call(bf16[16,640,128]{2,1,0:T(8,128)(2,1)} %bitcast.7, bf16[16,640,128]{2,1,0:T(8,128)(2,1)} %bitcast.8, bf16[16,640,128]{2,1,0:T(8,128)(2,1)} %bitcast.9, ...), custom_call_target="tpu_custom_call" | custom-call | tf_op jit(solution)/shard_map/temporal_attention_backward/pallas_call | solution.py:349
  209.0 3.3 %write_out.1 = (bf16[16,640,128]{2,1,0:T(8,128)(2,1)}, bf16[16,640,128]{2,1,0:T(8,128)(2,1)}, bf16[16,640,128]{2,1,0:T(8,128)(2,1)}, f32[5,128]{1,0:T(8,128)}, f32[5,128]{1,0:T(8,128)}) custom-call(bf16[16,640,128]{2,1,0:T(8,128)(2,1)S(1)} %get-tuple-element.14.oq, bf16[16,640,128]{2,1,0:T(8,128)(2,1)S(1)} %get-tuple-element.15.ok, ...), custom_call_target="tpu_custom_call" | custom-call | tf_op jit(solution)/shard_map/write_out/pallas_call | solution.py:394

commit v6 on v5

--- a/solution.py
+++ b/solution.py
@@ -39,6 +39,9 @@
     dp = lax.axis_index("dp")
     rows = q_hbm.shape[1]
     part = rows // CHUNKS
+    y, xh = lax.div(dp, 2), lax.rem(dp, 2)
+    sides = dp_size // 2
+    partner = 2 * y + 1 - xh
     local_heads = HEADS // dp_size
     pad = SEQ // 2
     scaling = 1.0 / math.sqrt(HDIM)
@@ -138,6 +141,7 @@
         lax.fori_loop(0, SEQ, one, 0)
 
     send_values(0)
+    send_values(1)
 
     @pl.when(me == 0)
     def _():
@@ -157,12 +161,16 @@
 
     for copy in gain_loads:
         copy.wait()
-    for step in range(1, dp_size):
-        remote_dp(
-            gsend, gbuf.at[dp], gain_send, gain_recv, lax.rem(dp + step, dp_size)
-        ).start()
-    pltpu.make_async_copy(gsend, gbuf.at[dp], gain_recv).start()
-    send_values(1)
+    remote_dp(gsend, gbuf.at[dp], gain_send.at[0], gain_recv.at[0], partner).start()
+    pltpu.make_async_copy(gsend, gbuf.at[dp], gain_recv.at[0]).start()
+    send_values(2)
+    both = gbuf.at[pl.ds(2 * y, 2)]
+    pltpu.make_async_copy(both, both, gain_recv.at[0]).wait()
+    for step in range(1, sides):
+        other = lax.rem(y + step, sides) * 2 + xh
+        remote_dp(both, both, gain_send.at[1], gain_recv.at[1], other).start()
+    for c in range(3, CHUNKS):
+        send_values(c)
 
     row_ids = lax.broadcasted_iota(jnp.int32, mask.shape, 0)
     col_ids = lax.broadcasted_iota(jnp.int32, mask.shape, 1)
@@ -170,7 +178,8 @@
     mask[...] = jnp.where(allowed, 0.0, NEGATIVE)
     acc[...] = jnp.zeros_like(acc)
 
-    pltpu.make_async_copy(gbuf, gbuf, gain_recv).wait()
+    rest = gbuf.at[pl.ds(0, dp_size - 2)]
+    pltpu.make_async_copy(rest, rest, gain_recv.at[1]).wait()
     for d in range(dp_size):
         for a in range(2):
             gain[a, d * local_heads : (d + 1) * local_heads] = gbuf[
@@ -179,10 +188,7 @@
     for copy in raw_loads:
         copy.wait()
 
-    send_normalized(0)
-    send_normalized(1)
-    for c in range(2, CHUNKS):
-        send_values(c)
+    for c in range(CHUNKS):
         send_normalized(c)
 
     def contract(left, right, dims):
@@ -305,10 +311,10 @@
     for a in range(2):
         pltpu.make_async_copy(oq.at[others], oq.at[others], ret_send.at[a]).wait()
     pltpu.make_async_copy(oq.at[others], oq.at[others], val_send).wait()
-    if dp_size > 1:
-        most = pl.ds(0, dp_size - 1)
-        pltpu.make_async_copy(gbuf.at[most], gbuf.at[most], gain_send).wait()
-        pltpu.make_async_copy(rbuf.at[most], rbuf.at[most], rs_send).wait()
+    pltpu.make_async_copy(gsend, gsend, gain_send.at[0]).wait()
+    pltpu.make_async_copy(rest, rest, gain_send.at[1]).wait()
+    most = rbuf.at[pl.ds(0, dp_size - 1)]
+    pltpu.make_async_copy(most, most, rs_send).wait()
     pltpu.make_async_copy(abuf.at[others], abuf.at[others], row_send).wait()
     pltpu.make_async_copy(bbuf.at[others], bbuf.at[others], ag_send).wait()
 
@@ -375,8 +381,8 @@
             dma((2, CHUNKS)),
             dma,
             dma,
-            dma,
-            dma,
+            dma((2,)),
+            dma((2,)),
             dma,
             dma,
             dma,

time: 212 us -> 211 us (level)
  no operation moved by 1% of the time
where the time goes in v6:
time: 211 us; the launch traced here: 210 us
  Pallas kernels  209 us (99%)
    pallas_call x1, Pallas kernels, body(): pl.pallas_call(functools.partial(kernel, dp_size), out_shape=(big, big, b...  206 us

profile of v6, /device:TPU:1, one launch (start us, length us, event | category | flops | bytes accessed | tf_op | source)
XLA Modules:
  0.0 210.4 jit_solution(6214947821679829928)
XLA Ops:
  0.6 0.7 select_maximum_fusion.gains_hbm
  1.3 205.8 %temporal_attention_backward.1 = (bf16[16,640,128]{2,1,0:T(8,128)(2,1)S(1)}, bf16[16,640,128]{2,1,0:T(8,128)(2,1)S(1)}, bf16[16,640,128]{2,1,0:T(8,128)(2,1)S(1)}, f32[16,128]{1,0:T(8,128)S(1)}) custom-call(bf16[16,640,128]{2,1,0:T(8,128)(2,1)} %bitcast.7, bf16[16,640,128]{2,1,0:T(8,128)(2,1)} %bitcast.8, bf16[16,640,128]{2,1,0:T(8,128)(2,1)} %bitcast.9, ...), custom_call_target="tpu_custom_call" | custom-call | tf_op jit(solution)/shard_map/temporal_attention_backward/pallas_call | solution.py:355
  207.1 3.3 %write_out.1 = (bf16[16,640,128]{2,1,0:T(8,128)(2,1)}, bf16[16,640,128]{2,1,0:T(8,128)(2,1)}, bf16[16,640,128]{2,1,0:T(8,128)(2,1)}, f32[5,128]{1,0:T(8,128)}, f32[5,128]{1,0:T(8,128)}) custom-call(bf16[16,640,128]{2,1,0:T(8,128)(2,1)S(1)} %get-tuple-element.14.oq, bf16[16,640,128]{2,1,0:T(8,128)(2,1)S(1)} %get-tuple-element.15.ok, ...), custom_call_target="tpu_custom_call" | custom-call | tf_op jit(solution)/shard_map/write_out/pallas_call | solution.py:400

commit v7 on v6

--- a/solution.py
+++ b/solution.py
@@ -19,7 +19,7 @@
 
 
 def peer_of(me, step):
-    step = lax.rem(step * 9, SEQ)
+    step = lax.rem(step * 7, SEQ)
     x = lax.rem(lax.div(me, 8) + lax.div(step, 8), 2)
     z = lax.rem(lax.div(me, 2) + lax.div(step, 2), 4)
     core = lax.rem(me + step, 2)
@@ -30,10 +30,10 @@
     dp_size,
     q_hbm, k_hbm, v_hbm, g_hbm, gains_hbm,
     oq, ok, ov, total_gain,
-    nrm, rcv, stg, ret, mask, gsend, gbuf, gain, acc, rsend, rbuf, asend, abuf, row, bbuf,
+    nrm, rcv, stg, ret, mask, gsend, gbuf, gain, acc, rsend, rbuf, asend, abuf, row, swapped, final, bbuf,
     raw_sem, load_sem, fwd_send, fwd_recv, ret_send, ret_recv, val_send, val_recv,
     gain_send, gain_recv, rs_send, rs_recv, row_send, row_recv, ag_send, ag_recv,
-    ready, everyone,
+    ready, everyone, swap_send, swap_recv,
 ):
     me = lax.axis_index("seq")
     dp = lax.axis_index("dp")
@@ -263,7 +263,7 @@
 
         lax.fori_loop(0, SEQ, one, 0)
 
-    lots = (0, CHUNKS // 4, CHUNKS // 2, 3 * CHUNKS // 4, CHUNKS)
+    lots = (0, 2, 4, 6, 7, CHUNKS)
 
     def send_lot(lot):
         for c in range(lots[lot], lots[lot + 1]):
@@ -282,25 +282,32 @@
             rsend[d, a * pad : a * pad + local_heads] = acc[
                 a, d * local_heads : (d + 1) * local_heads
             ]
-    for step in range(1, dp_size):
-        other = lax.rem(dp + step, dp_size)
-        remote_dp(rsend.at[other], rbuf.at[dp], rs_send, rs_recv, other).start()
-    pltpu.make_async_copy(rsend.at[dp], rbuf.at[dp], rs_recv).start()
+    for step in range(1, sides):
+        other = lax.rem(y + step, sides)
+        remote_dp(
+            rsend.at[pl.ds(2 * other, 2)], rbuf.at[y], rs_send, rs_recv, 2 * other + xh
+        ).start()
+    pltpu.make_async_copy(rsend.at[pl.ds(2 * y, 2)], rbuf.at[y], rs_recv).start()
     send_lot(1)
     pltpu.make_async_copy(rbuf, rbuf, rs_recv).wait()
     asend[...] = jnp.sum(rbuf[...], axis=0).reshape(asend.shape)
     for step in range(1, SEQ):
         seq = lax.rem(me + step, SEQ)
-        remote(asend.at[seq], abuf.at[me], row_send, row_recv, seq).start()
-    pltpu.make_async_copy(asend.at[me], abuf.at[me], row_recv).start()
+        remote(asend.at[:, seq], abuf.at[me], row_send, row_recv, seq).start()
+    pltpu.make_async_copy(asend.at[:, me], abuf.at[me], row_recv).start()
     send_lot(2)
     pltpu.make_async_copy(abuf, abuf, row_recv).wait()
     row[...] = jnp.sum(abuf[...], axis=0)
+    swap = remote_dp(row.at[1 - xh], swapped, swap_send, swap_recv, partner)
+    swap.start()
+    send_lot(3)
+    swap.wait()
+    final[...] = row[xh] + swapped[...]
     for step in range(1, SEQ):
         seq = lax.rem(me + step, SEQ)
-        remote(row, bbuf.at[me], ag_send, ag_recv, seq).start()
-    pltpu.make_async_copy(row, bbuf.at[me], ag_recv).start()
-    send_lot(3)
+        remote(final, bbuf.at[me], ag_send, ag_recv, seq).start()
+    pltpu.make_async_copy(final, bbuf.at[me], ag_recv).start()
+    send_lot(4)
     pltpu.make_async_copy(bbuf, bbuf, ag_recv).wait()
     total_gain[...] = bbuf[...].reshape(total_gain.shape)
 
@@ -313,7 +320,7 @@
     pltpu.make_async_copy(oq.at[others], oq.at[others], val_send).wait()
     pltpu.make_async_copy(gsend, gsend, gain_send.at[0]).wait()
     pltpu.make_async_copy(rest, rest, gain_send.at[1]).wait()
-    most = rbuf.at[pl.ds(0, dp_size - 1)]
+    most = rbuf.at[pl.ds(0, sides - 1)]
     pltpu.make_async_copy(most, most, rs_send).wait()
     pltpu.make_async_copy(abuf.at[others], abuf.at[others], row_send).wait()
     pltpu.make_async_copy(bbuf.at[others], bbuf.at[others], ag_send).wait()
@@ -368,9 +375,11 @@
             pltpu.VMEM((2, HEADS, HDIM), wide),
             pltpu.VMEM((2, HEADS, HDIM), wide),
             pltpu.VMEM((dp_size, 2 * pad, HDIM), wide),
-            pltpu.VMEM((dp_size, 2 * pad, HDIM), wide),
-            pltpu.VMEM((SEQ, 1, HDIM), wide),
-            pltpu.VMEM((SEQ, 1, HDIM), wide),
+            pltpu.VMEM((dp_size // 2, 2, 2 * pad, HDIM), wide),
+            pltpu.VMEM((2, SEQ, 1, HDIM), wide),
+            pltpu.VMEM((SEQ, 2, 1, HDIM), wide),
+            pltpu.VMEM((2, 1, HDIM), wide),
+            pltpu.VMEM((1, HDIM), wide),
             pltpu.VMEM((1, HDIM), wide),
             pltpu.VMEM((SEQ, 1, HDIM), wide),
             dma((2,)),
@@ -391,6 +400,8 @@
             dma,
             pltpu.SemaphoreType.REGULAR,
             pltpu.SemaphoreType.REGULAR,
+            dma,
+            dma,
         ],
         compiler_params=pltpu.CompilerParams(
             collective_id=0, has_side_effects=True, vmem_limit_bytes=44 * 2**20

time: 211 us -> 211 us (level)
  no operation moved by 1% of the time
where the time goes in v7:
time: 211 us
  Pallas kernels  210 us (100%)
    pallas_call x1, Pallas kernels, body(): pl.pallas_call(functools.partial(kernel, dp_size), out_shape=(big, big, b...  206 us

profile of v7, /device:TPU:1, one launch (start us, length us, event | category | flops | bytes accessed | tf_op | source)
XLA Modules:
  0.0 210.9 jit_solution(17888808455168381504)
XLA Ops:
  0.6 0.7 select_maximum_fusion.gains_hbm
  1.3 206.3 %temporal_attention_backward.1 = (bf16[16,640,128]{2,1,0:T(8,128)(2,1)S(1)}, bf16[16,640,128]{2,1,0:T(8,128)(2,1)S(1)}, bf16[16,640,128]{2,1,0:T(8,128)(2,1)S(1)}, f32[16,128]{1,0:T(8,128)S(1)}) custom-call(bf16[16,640,128]{2,1,0:T(8,128)(2,1)} %bitcast.7, bf16[16,640,128]{2,1,0:T(8,128)(2,1)} %bitcast.8, bf16[16,640,128]{2,1,0:T(8,128)(2,1)} %bitcast.9, ...), custom_call_target="tpu_custom_call" | custom-call | tf_op jit(solution)/shard_map/temporal_attention_backward/pallas_call | solution.py:362
  207.6 3.3 %write_out.1 = (bf16[16,640,128]{2,1,0:T(8,128)(2,1)}, bf16[16,640,128]{2,1,0:T(8,128)(2,1)}, bf16[16,640,128]{2,1,0:T(8,128)(2,1)}, f32[5,128]{1,0:T(8,128)}, f32[5,128]{1,0:T(8,128)}) custom-call(bf16[16,640,128]{2,1,0:T(8,128)(2,1)S(1)} %get-tuple-element.14.oq, bf16[16,640,128]{2,1,0:T(8,128)(2,1)S(1)} %get-tuple-element.15.ok, ...), custom_call_target="tpu_custom_call" | custom-call | tf_op jit(solution)/shard_map/write_out/pallas_call | solution.py:411

commit v8 on v7

--- a/solution.py
+++ b/solution.py
@@ -19,7 +19,7 @@
 
 
 def peer_of(me, step):
-    step = lax.rem(step * 7, SEQ)
+    step = lax.rem(step * 13, SEQ)
     x = lax.rem(lax.div(me, 8) + lax.div(step, 8), 2)
     z = lax.rem(lax.div(me, 2) + lax.div(step, 2), 4)
     core = lax.rem(me + step, 2)

time: 211 us -> 210 us (level)
  no operation moved by 1% of the time
where the time goes in v8:
time: 210 us
  Pallas kernels  209 us (100%)
    pallas_call x1, Pallas kernels, body(): pl.pallas_call(functools.partial(kernel, dp_size), out_shape=(big, big, b...  206 us

profile of v8, /device:TPU:1, one launch (start us, length us, event | category | flops | bytes accessed | tf_op | source)
XLA Modules:
  0.0 210.3 jit_solution(10304093157226611259)
XLA Ops:
  0.6 0.7 select_maximum_fusion.gains_hbm
  1.3 205.7 %temporal_attention_backward.1 = (bf16[16,640,128]{2,1,0:T(8,128)(2,1)S(1)}, bf16[16,640,128]{2,1,0:T(8,128)(2,1)S(1)}, bf16[16,640,128]{2,1,0:T(8,128)(2,1)S(1)}, f32[16,128]{1,0:T(8,128)S(1)}) custom-call(bf16[16,640,128]{2,1,0:T(8,128)(2,1)} %bitcast.7, bf16[16,640,128]{2,1,0:T(8,128)(2,1)} %bitcast.8, bf16[16,640,128]{2,1,0:T(8,128)(2,1)} %bitcast.9, ...), custom_call_target="tpu_custom_call" | custom-call | tf_op jit(solution)/shard_map/temporal_attention_backward/pallas_call | solution.py:362
  207.0 3.3 %write_out.1 = (bf16[16,640,128]{2,1,0:T(8,128)(2,1)}, bf16[16,640,128]{2,1,0:T(8,128)(2,1)}, bf16[16,640,128]{2,1,0:T(8,128)(2,1)}, f32[5,128]{1,0:T(8,128)}, f32[5,128]{1,0:T(8,128)}) custom-call(bf16[16,640,128]{2,1,0:T(8,128)(2,1)S(1)} %get-tuple-element.14.oq, bf16[16,640,128]{2,1,0:T(8,128)(2,1)S(1)} %get-tuple-element.15.ok, ...), custom_call_target="tpu_custom_call" | custom-call | tf_op jit(solution)/shard_map/write_out/pallas_call | solution.py:411

commit v9 on v8

--- a/solution.py
+++ b/solution.py
@@ -261,7 +261,7 @@
                 acc[a] += jnp.sum((step * hat).reshape(part // HEADS, HEADS, HDIM), axis=0)
             return carry
 
-        lax.fori_loop(0, SEQ, one, 0)
+        lax.fori_loop(0, SEQ, one, 0, unroll=4)
 
     lots = (0, 2, 4, 6, 7, CHUNKS)
 

time: 210 us -> 210 us (level)
  no operation moved by 1% of the time
where the time goes in v9:
time: 210 us
  Pallas kernels  209 us (100%)
    pallas_call x1, Pallas kernels, body(): pl.pallas_call(functools.partial(kernel, dp_size), out_shape=(big, big, b...  206 us

profile of v9, /device:TPU:1, one launch (start us, length us, event | category | flops | bytes accessed | tf_op | source)
XLA Modules:
  0.0 210.3 jit_solution(4874309972994005409)
XLA Ops:
  0.6 0.7 select_maximum_fusion.gains_hbm
  1.3 205.7 %temporal_attention_backward.1 = (bf16[16,640,128]{2,1,0:T(8,128)(2,1)S(1)}, bf16[16,640,128]{2,1,0:T(8,128)(2,1)S(1)}, bf16[16,640,128]{2,1,0:T(8,128)(2,1)S(1)}, f32[16,128]{1,0:T(8,128)S(1)}) custom-call(bf16[16,640,128]{2,1,0:T(8,128)(2,1)} %bitcast.7, bf16[16,640,128]{2,1,0:T(8,128)(2,1)} %bitcast.8, bf16[16,640,128]{2,1,0:T(8,128)(2,1)} %bitcast.9, ...), custom_call_target="tpu_custom_call" | custom-call | tf_op jit(solution)/shard_map/temporal_attention_backward/pallas_call | solution.py:362
  207.0 3.3 %write_out.1 = (bf16[16,640,128]{2,1,0:T(8,128)(2,1)}, bf16[16,640,128]{2,1,0:T(8,128)(2,1)}, bf16[16,640,128]{2,1,0:T(8,128)(2,1)}, f32[5,128]{1,0:T(8,128)}, f32[5,128]{1,0:T(8,128)}) custom-call(bf16[16,640,128]{2,1,0:T(8,128)(2,1)S(1)} %get-tuple-element.14.oq, bf16[16,640,128]{2,1,0:T(8,128)(2,1)S(1)} %get-tuple-element.15.ok, ...), custom_call_target="tpu_custom_call" | custom-call | tf_op jit(solution)/shard_map/write_out/pallas_call | solution.py:411
